TPU v7x, 768 devices: a whole 4x8x12 slice. The times are simulated.
768 devices in a mesh: ctx: 32 (over y, z_lo), head: 24 (over z_hi, x, core).
Axes of the slice: x: 4, y: 8, z: 12 (z_hi: 3, z_lo: 4; z = z_hi * 4 + z_lo), core: 2. Of those that a mesh axis runs over, the one named last changes fastest.
Arguments:
- queries: bfloat16 [16384, 96, 128], P('ctx', 'head'), may hold values from -16 to 16
- keys: bfloat16 [16384, 6, 128], P('ctx'), may hold values from -6 to 6
- values: bfloat16 [16384, 6, 128], P('ctx'), may hold values from -6 to 6
- d_out: bfloat16 [16384, 96, 128], P('ctx', 'head'), may hold values from -1.796875 to 1.796875
- block_pos: int32 [4, 32], replicated, may hold values from 0 to 31, each once within a row
- block_mask: int32 [4, 32, 32], replicated, may hold values 0 or 1
Outputs:
- d_queries: bfloat16 [16384, 96, 128], P('ctx', 'head')
- d_keys: bfloat16 [16384, 6, 128], P('ctx')
- d_values: bfloat16 [16384, 6, 128], P('ctx')
Inputs may be any that keep to these rules, and one draw needn't show every extreme that they name: `block_pos`: each row holds each of the 32 block numbers once. `block_mask`: only entries [s, i, i2] with i2 < i are read.
All inputs are finite; a program needn't handle non-finite values.
Results may differ from a plain program's by a relative error of at most 0.0075.
Values may be sent and summed in bfloat16 or wider, within the bound.
A program may use at most 32 MiB of HBM per device.

v0:
```python
import jax
import jax.numpy as jnp
from jax import lax
from jax.sharding import PartitionSpec as P

GROUP = 16
BLK = 128
SEQS = 4
QB_DEV = 4


def shifted(value, axis, steps):
    count = lax.axis_size(axis)
    pairs = [(source, (source + steps) % count) for source in range(count)]
    return lax.ppermute(value, axis, pairs)


def contract_last(left, right):
    return lax.dot_general(
        left, right, (((1,), (1,)), ((), ())), preferred_element_type=jnp.float32
    )


def contract_first(left, right):
    return lax.dot_general(
        left, right, (((0,), (0,)), ((), ())), preferred_element_type=jnp.float32
    )


def pass_keys(key_pair):
    return shifted(key_pair, "ctx", SEQS)


def send_sums(key_sums):
    return shifted(key_sums, "ctx", SEQS)


def per_device(queries, keys, values, d_out, block_pos, block_mask):
    cycle_members = lax.axis_size("ctx") // SEQS
    head_dim = queries.shape[2]
    score_scale = head_dim ** (-0.5)
    shard_tokens = queries.shape[0]
    local_heads = queries.shape[1]
    kv_count = keys.shape[1]
    kv_index = lax.axis_index("head") * local_heads // GROUP
    key_local = lax.dynamic_index_in_dim(keys, kv_index, 1, keepdims=False)
    value_local = lax.dynamic_index_in_dim(values, kv_index, 1, keepdims=False)
    row_total = shard_tokens * local_heads
    query_rows = queries.reshape(row_total, head_dim)
    grad_rows = d_out.reshape(row_total, head_dim)
    own_pair = jnp.stack([key_local, value_local])
    ctx_index = lax.axis_index("ctx")
    seq_id = ctx_index % SEQS
    member = ctx_index // SEQS
    order_row = lax.dynamic_index_in_dim(block_pos, seq_id, 0, keepdims=False)
    mask_table = lax.dynamic_index_in_dim(block_mask, seq_id, 0, keepdims=False)

    def blocks_of(owner_member):
        return lax.dynamic_slice_in_dim(order_row, owner_member % cycle_members * QB_DEV, QB_DEV)

    query_blocks = blocks_of(member)
    query_offset = lax.broadcasted_iota(jnp.int32, (1, BLK, 1, 1, 1), 1)
    key_offset = lax.broadcasted_iota(jnp.int32, (1, 1, 1, 1, BLK), 4)
    causal = key_offset <= query_offset

    def hop_mask(owner_member):
        key_blocks = blocks_of(owner_member)
        query_ids = query_blocks[:, None]
        key_ids = key_blocks[None, :]
        entries = mask_table[query_ids, key_ids]
        earlier = jnp.logical_and(key_ids < query_ids, entries == 1)
        same = query_ids == key_ids
        allowed = jnp.logical_or(
            earlier[:, None, None, :, None], jnp.logical_and(same[:, None, None, :, None], causal)
        )
        allowed = jnp.broadcast_to(allowed, (QB_DEV, BLK, local_heads, QB_DEV, BLK))
        active = jnp.any(jnp.logical_or(earlier, same))
        return (allowed.reshape(row_total, shard_tokens), active)

    def masked_logits(key_pair, allowed):
        logits = contract_last(query_rows, key_pair[0]) * score_scale
        return jnp.where(allowed, logits, -jnp.inf)

    def add_stats(running, key_pair, owner_member):
        allowed, active = hop_mask(owner_member)

        def update(running):
            maxima, totals, weighted = running
            logits = masked_logits(key_pair, allowed)
            dprob_rows = contract_last(grad_rows, key_pair[1])
            new_max = jnp.maximum(maxima, jnp.max(logits, axis=1))
            factor = jnp.exp(maxima - new_max)
            exp_rows = jnp.exp(logits - new_max[:, None])
            return (
                new_max,
                totals * factor + jnp.sum(exp_rows, axis=1),
                weighted * factor + jnp.sum(exp_rows * dprob_rows, axis=1),
            )

        return lax.cond(active, update, lambda kept: kept, running)

    kept_pairs = None
    stats = (
        jnp.full((row_total,), -jnp.inf, jnp.float32),
        jnp.zeros((row_total,), jnp.float32),
        jnp.zeros((row_total,), jnp.float32),
    )
    stats = add_stats(stats, own_pair, member)

    def one_way(hop_index, loop_state):
        stats, key_pair, kept_pairs = loop_state
        key_pair = pass_keys(key_pair)
        stats = add_stats(stats, key_pair, member - hop_index - 1)
        return (stats, key_pair, kept_pairs)

    stats, last_pair, kept_pairs = lax.fori_loop(
        0, cycle_members - 1, one_way, (stats, own_pair, kept_pairs)
    )
    maxima, totals, weighted = stats
    log_sums = maxima + jnp.log(totals)
    deltas = weighted / totals

    def add_grads(running, key_pair, owner_member):
        allowed, active = hop_mask(owner_member)

        def update(running):
            query_grad, key_sums = running
            logits = masked_logits(key_pair, allowed)
            prob_rows = jnp.exp(logits - log_sums[:, None])
            dprob_rows = contract_last(grad_rows, key_pair[1])
            dscore = (prob_rows * (dprob_rows - deltas[:, None])).astype(jnp.bfloat16)
            query_grad = query_grad + jnp.dot(
                dscore, key_pair[0], preferred_element_type=jnp.float32
            )
            key_add = contract_first(dscore, query_rows)
            value_add = contract_first(prob_rows.astype(jnp.bfloat16), grad_rows)
            return (query_grad, key_sums + jnp.stack([key_add, value_add]))

        return lax.cond(active, update, lambda kept: kept, running)

    query_grad = jnp.zeros((row_total, head_dim), jnp.float32)
    key_sums = jnp.zeros((2, shard_tokens, head_dim), jnp.float32)

    def resend_step(hop_index, loop_state):
        query_grad, key_sums, key_pair = loop_state
        query_grad, key_sums = add_grads((query_grad, key_sums), key_pair, member - hop_index)
        return (query_grad, send_sums(key_sums), pass_keys(key_pair))

    query_grad, key_sums, key_pair = lax.fori_loop(
        0, cycle_members - 1, resend_step, (query_grad, key_sums, own_pair)
    )
    query_grad, key_sums = add_grads((query_grad, key_sums), key_pair, member - (cycle_members - 1))
    key_sums = send_sums(key_sums)
    d_queries = (
        (query_grad * score_scale).reshape(shard_tokens, local_heads, head_dim).astype(jnp.bfloat16)
    )
    slot_weight = (lax.broadcasted_iota(jnp.int32, (kv_count,), 0) == kv_index).astype(jnp.float32)
    scaled = jnp.stack([key_sums[0] * score_scale, key_sums[1]])
    spread = scaled[:, :, None, :] * slot_weight[None, None, :, None]
    summed = lax.psum(spread, "head")
    return (d_queries, summed[0].astype(jnp.bfloat16), summed[1].astype(jnp.bfloat16))


def solution(mesh):
    placed = (
        P("ctx", "head", None),
        P("ctx", None, None),
        P("ctx", None, None),
        P("ctx", "head", None),
        P(),
        P(),
    )
    return jax.shard_map(
        per_device,
        mesh=mesh,
        in_specs=placed,
        out_specs=(P("ctx", "head", None), P("ctx", None, None), P("ctx", None, None)),
        check_vma=False,
    )
```

profile of v0, /device:TPU:1, one launch (start us, length us, event | category | flops | bytes accessed | tf_op | source)
XLA Modules:
  0.0 532.1 jit_solution(11887404719389056345)
XLA Ops:
  8.2 7.8 %conditional.4 = (f32[2048]{0:T(1024)}, f32[2048]{0:T(1024)S(1)}, f32[2048]{0:T(1024)S(1)}) conditional(s32[]{:T(128)} %convert_element_type.66, () %tuple.103, (s32[4]{0:T(128)S(1)}, s32[4,1,1,4,1]{3,0,4,2,1:T(4,128)S(1)}, s32[4,4]{1,0:T(4,128)S(1)}, s32[4,1,1,4,1]{3,0,4,2,1:T(4,128)S(1)}, pred[4,128,1,4,128]{4,3,1,0,2:T(4,128)(4,1)S(1)}, ...), branch_computations={%region_2.3_spmd, %region_3.7_spmd} | conditional | flops 545785920 | bytes 21053736 | solution.py:100
  16.0 113.8 %while.42 = (s32[]{:T(128)}, f32[2048]{0:T(1024)}, f32[2048]{0:T(1024)S(1)}, f32[2048]{0:T(1024)S(1)}, bf16[2,512,128]{2,1,0:T(8,128)(2,1)S(1)}, /*index=5*/s32[...) while((s32[]{:T(128)}, f32[2048]{0:T(1024)}, ...), condition=%wide.region_14.15_spmd.clone, body=%wide.region_7.0_spmd.clone.sunk | while | flops 545806592 | bytes 22726088 | solution.py:116
  25.7 7.2 %conditional.10 = ((f32[2048]{0:T(1024)}, f32[2048]{0:T(1024)S(1)}, f32[2048]{0:T(1024)S(1)})) conditional(s32[]{:T(128)} %convert_element_type.88, (f32[2048]{0:T(1024)}, f32[2048]{0:T(1024)S(1)}, f32[2048]{0:T(1024)S(1)}) %tuple.165, (s32[4]{0:T(128)S(1)}, s32[4]{0:T(128)S(1)}, s32[4,4]{1,0:T(4,128)S(1)}, s32[1,128,1,1,128]{4,1,3,2,0:T(8,128)S(1)}, ...), branch_computations={%region_9.9_spmd, %region_10.13_spmd} | conditional | flops 545806400 | bytes 21020864 | solution.py:100
  42.0 7.2 %conditional.10 = ((f32[2048]{0:T(1024)}, f32[2048]{0:T(1024)S(1)}, f32[2048]{0:T(1024)S(1)})) conditional(s32[]{:T(128)} %convert_element_type.88, (f32[2048]{0:T(1024)}, f32[2048]{0:T(1024)S(1)}, f32[2048]{0:T(1024)S(1)}) %tuple.165, (s32[4]{0:T(128)S(1)}, s32[4]{0:T(128)S(1)}, s32[4,4]{1,0:T(4,128)S(1)}, s32[1,128,1,1,128]{4,1,3,2,0:T(8,128)S(1)}, ...), branch_computations={%region_9.9_spmd, %region_10.13_spmd} | conditional | flops 545806400 | bytes 21020864 | solution.py:100
  57.7 7.2 %conditional.10 = ((f32[2048]{0:T(1024)}, f32[2048]{0:T(1024)S(1)}, f32[2048]{0:T(1024)S(1)})) conditional(s32[]{:T(128)} %convert_element_type.88, (f32[2048]{0:T(1024)}, f32[2048]{0:T(1024)S(1)}, f32[2048]{0:T(1024)S(1)}) %tuple.165, (s32[4]{0:T(128)S(1)}, s32[4]{0:T(128)S(1)}, s32[4,4]{1,0:T(4,128)S(1)}, s32[1,128,1,1,128]{4,1,3,2,0:T(8,128)S(1)}, ...), branch_computations={%region_9.9_spmd, %region_10.13_spmd} | conditional | flops 545806400 | bytes 21020864 | solution.py:100
  73.3 7.2 %conditional.10 = ((f32[2048]{0:T(1024)}, f32[2048]{0:T(1024)S(1)}, f32[2048]{0:T(1024)S(1)})) conditional(s32[]{:T(128)} %convert_element_type.88, (f32[2048]{0:T(1024)}, f32[2048]{0:T(1024)S(1)}, f32[2048]{0:T(1024)S(1)}) %tuple.165, (s32[4]{0:T(128)S(1)}, s32[4]{0:T(128)S(1)}, s32[4,4]{1,0:T(4,128)S(1)}, s32[1,128,1,1,128]{4,1,3,2,0:T(8,128)S(1)}, ...), branch_computations={%region_9.9_spmd, %region_10.13_spmd} | conditional | flops 545806400 | bytes 21020864 | solution.py:100
  88.9 7.2 %conditional.10 = ((f32[2048]{0:T(1024)}, f32[2048]{0:T(1024)S(1)}, f32[2048]{0:T(1024)S(1)})) conditional(s32[]{:T(128)} %convert_element_type.88, (f32[2048]{0:T(1024)}, f32[2048]{0:T(1024)S(1)}, f32[2048]{0:T(1024)S(1)}) %tuple.165, (s32[4]{0:T(128)S(1)}, s32[4]{0:T(128)S(1)}, s32[4,4]{1,0:T(4,128)S(1)}, s32[1,128,1,1,128]{4,1,3,2,0:T(8,128)S(1)}, ...), branch_computations={%region_9.9_spmd, %region_10.13_spmd} | conditional | flops 545806400 | bytes 21020864 | solution.py:100
  105.1 7.2 %conditional.10 = ((f32[2048]{0:T(1024)}, f32[2048]{0:T(1024)S(1)}, f32[2048]{0:T(1024)S(1)})) conditional(s32[]{:T(128)} %convert_element_type.88, (f32[2048]{0:T(1024)}, f32[2048]{0:T(1024)S(1)}, f32[2048]{0:T(1024)S(1)}) %tuple.165, (s32[4]{0:T(128)S(1)}, s32[4]{0:T(128)S(1)}, s32[4,4]{1,0:T(4,128)S(1)}, s32[1,128,1,1,128]{4,1,3,2,0:T(8,128)S(1)}, ...), branch_computations={%region_9.9_spmd, %region_10.13_spmd} | conditional | flops 545806400 | bytes 21020864 | solution.py:100
  116.7 5.8 %collective-permute-done = bf16[2,512,128]{2,1,0:T(8,128)(2,1)S(1)} collective-permute-done((bf16[2,512,128]{2,1,0:T(8,128)(2,1)S(1)}, bf16[2,512,128]{2,1,0:T(8,128)(2,1)S(1)}, u32[]{:S(2)}, u32[]{:S(2)}) %collective-permute-start) | collective-permute-done | bytes 262176 | tf_op jit(solution)/shard_map/while/body/eval_jaxpr/ppermute | solution.py:15
  122.5 7.2 %conditional.10 = ((f32[2048]{0:T(1024)}, f32[2048]{0:T(1024)S(1)}, f32[2048]{0:T(1024)S(1)})) conditional(s32[]{:T(128)} %convert_element_type.88, (f32[2048]{0:T(1024)}, f32[2048]{0:T(1024)S(1)}, f32[2048]{0:T(1024)S(1)}) %tuple.165, (s32[4]{0:T(128)S(1)}, s32[4]{0:T(128)S(1)}, s32[4,4]{1,0:T(4,128)S(1)}, s32[1,128,1,1,128]{4,1,3,2,0:T(8,128)S(1)}, ...), branch_computations={%region_9.9_spmd, %region_10.13_spmd} | conditional | flops 545806400 | bytes 21020864 | solution.py:100
  130.6 189.3 %while.43 = (s32[]{:T(128)}, f32[2048,128]{1,0:T(8,128)S(1)}, f32[2,512,128]{2,1,0:T(8,128)S(1)}, bf16[2,512,128]{2,1,0:T(8,128)(2,1)S(1)}, s32[]{:T(128)}, /*in...) while((s32[]{:T(128)}, f32[2048,128]{1,0:T(8,128)S(1)}, ...), condition=%wide.region_19.20_spmd.clone, body=%wide.region_15.19_spmd.clone.sunk | while | flops 1350582400 | bytes 33211868 | solution.py:149
  142.4 7.4 %collective-permute-done.1 = f32[2,512,128]{2,1,0:T(8,128)} collective-permute-done((f32[2,512,128]{2,1,0:T(8,128)S(1)}, f32[2,512,128]{2,1,0:T(8,128)}, u32[]{:S(2)}, u32[]{:S(2)}) %collective-permute-start.1) | collective-permute-done | bytes 524320 | tf_op jit(solution)/shard_map/while/body/eval_jaxpr/ppermute | solution.py:15
  164.3 10.8 %collective-permute-done.1 = f32[2,512,128]{2,1,0:T(8,128)} collective-permute-done((f32[2,512,128]{2,1,0:T(8,128)S(1)}, f32[2,512,128]{2,1,0:T(8,128)}, u32[]{:S(2)}, u32[]{:S(2)}) %collective-permute-start.1) | collective-permute-done | bytes 524320 | tf_op jit(solution)/shard_map/while/body/eval_jaxpr/ppermute | solution.py:15
  180.2 5.5 %conditional.11 = ((f32[2048,128]{1,0:T(8,128)S(1)}, f32[2,512,128]{2,1,0:T(8,128)S(1)})) conditional(s32[]{:T(128)} %convert_element_type.89, (f32[2048,128]{1,0:T(8,128)S(1)}, f32[2,512,128]{2,1,0:T(8,128)S(1)}) %tuple.169, (s32[4]{0:T(128)S(1)}, s32[4]{0:T(128)S(1)}, s32[4,4]{1,0:T(4,128)S(1)}, s32[1,128,1,1,128]{4,1,3,2,0:T(8,128)S(1)}, ...), branch_computations={%region_17.17_spmd, %region_18.18_spmd} | conditional | flops 1350582272 | bytes 28360888 | solution.py:139
  189.6 11.9 %collective-permute-done.1 = f32[2,512,128]{2,1,0:T(8,128)} collective-permute-done((f32[2,512,128]{2,1,0:T(8,128)S(1)}, f32[2,512,128]{2,1,0:T(8,128)}, u32[]{:S(2)}, u32[]{:S(2)}) %collective-permute-start.1) | collective-permute-done | bytes 524320 | tf_op jit(solution)/shard_map/while/body/eval_jaxpr/ppermute | solution.py:15
  206.5 5.5 %conditional.11 = ((f32[2048,128]{1,0:T(8,128)S(1)}, f32[2,512,128]{2,1,0:T(8,128)S(1)})) conditional(s32[]{:T(128)} %convert_element_type.89, (f32[2048,128]{1,0:T(8,128)S(1)}, f32[2,512,128]{2,1,0:T(8,128)S(1)}) %tuple.169, (s32[4]{0:T(128)S(1)}, s32[4]{0:T(128)S(1)}, s32[4,4]{1,0:T(4,128)S(1)}, s32[1,128,1,1,128]{4,1,3,2,0:T(8,128)S(1)}, ...), branch_computations={%region_17.17_spmd, %region_18.18_spmd} | conditional | flops 1350582272 | bytes 28360888 | solution.py:139
  215.9 13.0 %collective-permute-done.1 = f32[2,512,128]{2,1,0:T(8,128)} collective-permute-done((f32[2,512,128]{2,1,0:T(8,128)S(1)}, f32[2,512,128]{2,1,0:T(8,128)}, u32[]{:S(2)}, u32[]{:S(2)}) %collective-permute-start.1) | collective-permute-done | bytes 524320 | tf_op jit(solution)/shard_map/while/body/eval_jaxpr/ppermute | solution.py:15
  243.3 13.3 %collective-permute-done.1 = f32[2,512,128]{2,1,0:T(8,128)} collective-permute-done((f32[2,512,128]{2,1,0:T(8,128)S(1)}, f32[2,512,128]{2,1,0:T(8,128)}, u32[]{:S(2)}, u32[]{:S(2)}) %collective-permute-start.1) | collective-permute-done | bytes 524320 | tf_op jit(solution)/shard_map/while/body/eval_jaxpr/ppermute | solution.py:15
  262.5 5.5 %conditional.11 = ((f32[2048,128]{1,0:T(8,128)S(1)}, f32[2,512,128]{2,1,0:T(8,128)S(1)})) conditional(s32[]{:T(128)} %convert_element_type.89, (f32[2048,128]{1,0:T(8,128)S(1)}, f32[2,512,128]{2,1,0:T(8,128)S(1)}) %tuple.169, (s32[4]{0:T(128)S(1)}, s32[4]{0:T(128)S(1)}, s32[4,4]{1,0:T(4,128)S(1)}, s32[1,128,1,1,128]{4,1,3,2,0:T(8,128)S(1)}, ...), branch_computations={%region_17.17_spmd, %region_18.18_spmd} | conditional | flops 1350582272 | bytes 28360888 | solution.py:139
  271.8 13.1 %collective-permute-done.1 = f32[2,512,128]{2,1,0:T(8,128)} collective-permute-done((f32[2,512,128]{2,1,0:T(8,128)S(1)}, f32[2,512,128]{2,1,0:T(8,128)}, u32[]{:S(2)}, u32[]{:S(2)}) %collective-permute-start.1) | collective-permute-done | bytes 524320 | tf_op jit(solution)/shard_map/while/body/eval_jaxpr/ppermute | solution.py:15
  292.1 5.5 %conditional.11 = ((f32[2048,128]{1,0:T(8,128)S(1)}, f32[2,512,128]{2,1,0:T(8,128)S(1)})) conditional(s32[]{:T(128)} %convert_element_type.89, (f32[2048,128]{1,0:T(8,128)S(1)}, f32[2,512,128]{2,1,0:T(8,128)S(1)}) %tuple.169, (s32[4]{0:T(128)S(1)}, s32[4]{0:T(128)S(1)}, s32[4,4]{1,0:T(4,128)S(1)}, s32[1,128,1,1,128]{4,1,3,2,0:T(8,128)S(1)}, ...), branch_computations={%region_17.17_spmd, %region_18.18_spmd} | conditional | flops 1350582272 | bytes 28360888 | solution.py:139
  301.4 12.9 %collective-permute-done.1 = f32[2,512,128]{2,1,0:T(8,128)} collective-permute-done((f32[2,512,128]{2,1,0:T(8,128)S(1)}, f32[2,512,128]{2,1,0:T(8,128)}, u32[]{:S(2)}, u32[]{:S(2)}) %collective-permute-start.1) | collective-permute-done | bytes 524320 | tf_op jit(solution)/shard_map/while/body/eval_jaxpr/ppermute | solution.py:15
  328.1 10.5 %collective-permute-done.3 = f32[2,512,128]{2,1,0:T(8,128)S(1)} collective-permute-done((f32[2,512,128]{2,1,0:T(8,128)S(1)}, f32[2,512,128]{2,1,0:T(8,128)S(1)}, u32[]{:S(2)}, u32[]{:S(2)}) %collective-permute-start.3) | collective-permute-done | bytes 524320 | tf_op jit(solution)/shard_map/ppermute | solution.py:15
  339.0 190.5 %all-reduce.1 = bf16[2,512,6,128]{3,1,2,0:T(8,128)(2,1)} all-reduce(f32[2,512,6,128]{3,1,2,0:T(8,128)S(1)} %broadcast_multiply_fusion), channel_id=1, replica_groups=mesh['ctx'=32,'head'=24] {'head'}, use_global_device_ids=true, to_apply=%region_22.23 | all-reduce | flops 786432 | bytes 4718592 | tf_op jit(solution)/shard_map/psum | solution.py:160
  (378 shorter events, 251.8 us)
Async XLA Ops:
  0.6 7.5 %copy-start.1 = (bf16[512,4,128]{2,1,0:T(4,128)(2,1)S(1)}, bf16[512,4,128]{2,1,0:T(4,128)(2,1)}, u32[]{:S(2)}) copy-start(bf16[512,4,128]{2,1,0:T(4,128)(2,1)} %param.21) | copy-start | bytes 1572868
  0.7 7.5 %copy-start.2 = (bf16[512,4,128]{2,1,0:T(4,128)(2,1)S(1)}, bf16[512,4,128]{2,1,0:T(4,128)(2,1)}, u32[]{:S(2)}) copy-start(bf16[512,4,128]{2,1,0:T(4,128)(2,1)} %param.18) | copy-start | bytes 1572868
  16.0 9.7 %collective-permute-start = (bf16[2,512,128]{2,1,0:T(8,128)(2,1)S(1)}, bf16[2,512,128]{2,1,0:T(8,128)(2,1)S(1)}, u32[]{:S(2)}, u32[]{:S(2)}) collective-permute-start(bf16[2,512,128]{2,1,0:T(8,128)(2,1)S(1)} %get-tuple-element.1370), channel_id=1, source_target_pairs={{0,96},{24,120},{48,144},{72,168},{96,192},{120,216},{144,240},{16... | collective-permute-start | bytes 786440 | tf_op jit(solution)/shard_map/while/body/eval_jaxpr/ppermute | solution.py:15
  33.0 9.1 %collective-permute-start = (bf16[2,512,128]{2,1,0:T(8,128)(2,1)S(1)}, bf16[2,512,128]{2,1,0:T(8,128)(2,1)S(1)}, u32[]{:S(2)}, u32[]{:S(2)}) collective-permute-start(bf16[2,512,128]{2,1,0:T(8,128)(2,1)S(1)} %get-tuple-element.1370), channel_id=1, source_target_pairs={{0,96},{24,120},{48,144},{72,168},{96,192},{120,216},{144,240},{16... | collective-permute-start | bytes 786440 | tf_op jit(solution)/shard_map/while/body/eval_jaxpr/ppermute | solution.py:15
  49.3 8.3 %collective-permute-start = (bf16[2,512,128]{2,1,0:T(8,128)(2,1)S(1)}, bf16[2,512,128]{2,1,0:T(8,128)(2,1)S(1)}, u32[]{:S(2)}, u32[]{:S(2)}) collective-permute-start(bf16[2,512,128]{2,1,0:T(8,128)(2,1)S(1)} %get-tuple-element.1370), channel_id=1, source_target_pairs={{0,96},{24,120},{48,144},{72,168},{96,192},{120,216},{144,240},{16... | collective-permute-start | bytes 786440 | tf_op jit(solution)/shard_map/while/body/eval_jaxpr/ppermute | solution.py:15
  64.9 8.3 %collective-permute-start = (bf16[2,512,128]{2,1,0:T(8,128)(2,1)S(1)}, bf16[2,512,128]{2,1,0:T(8,128)(2,1)S(1)}, u32[]{:S(2)}, u32[]{:S(2)}) collective-permute-start(bf16[2,512,128]{2,1,0:T(8,128)(2,1)S(1)} %get-tuple-element.1370), channel_id=1, source_target_pairs={{0,96},{24,120},{48,144},{72,168},{96,192},{120,216},{144,240},{16... | collective-permute-start | bytes 786440 | tf_op jit(solution)/shard_map/while/body/eval_jaxpr/ppermute | solution.py:15
  80.5 8.3 %collective-permute-start = (bf16[2,512,128]{2,1,0:T(8,128)(2,1)S(1)}, bf16[2,512,128]{2,1,0:T(8,128)(2,1)S(1)}, u32[]{:S(2)}, u32[]{:S(2)}) collective-permute-start(bf16[2,512,128]{2,1,0:T(8,128)(2,1)S(1)} %get-tuple-element.1370), channel_id=1, source_target_pairs={{0,96},{24,120},{48,144},{72,168},{96,192},{120,216},{144,240},{16... | collective-permute-start | bytes 786440 | tf_op jit(solution)/shard_map/while/body/eval_jaxpr/ppermute | solution.py:15
  96.1 9.0 %collective-permute-start = (bf16[2,512,128]{2,1,0:T(8,128)(2,1)S(1)}, bf16[2,512,128]{2,1,0:T(8,128)(2,1)S(1)}, u32[]{:S(2)}, u32[]{:S(2)}) collective-permute-start(bf16[2,512,128]{2,1,0:T(8,128)(2,1)S(1)} %get-tuple-element.1370), channel_id=1, source_target_pairs={{0,96},{24,120},{48,144},{72,168},{96,192},{120,216},{144,240},{16... | collective-permute-start | bytes 786440 | tf_op jit(solution)/shard_map/while/body/eval_jaxpr/ppermute | solution.py:15
  112.4 10.1 %collective-permute-start = (bf16[2,512,128]{2,1,0:T(8,128)(2,1)S(1)}, bf16[2,512,128]{2,1,0:T(8,128)(2,1)S(1)}, u32[]{:S(2)}, u32[]{:S(2)}) collective-permute-start(bf16[2,512,128]{2,1,0:T(8,128)(2,1)S(1)} %get-tuple-element.1370), channel_id=1, source_target_pairs={{0,96},{24,120},{48,144},{72,168},{96,192},{120,216},{144,240},{16... | collective-permute-start | bytes 786440 | tf_op jit(solution)/shard_map/while/body/eval_jaxpr/ppermute | solution.py:15
  138.6 11.2 %collective-permute-start.1 = (f32[2,512,128]{2,1,0:T(8,128)S(1)}, f32[2,512,128]{2,1,0:T(8,128)}, u32[]{:S(2)}, u32[]{:S(2)}) collective-permute-start(f32[2,512,128]{2,1,0:T(8,128)S(1)} %get-tuple-element.1331), channel_id=1, source_target_pairs={{0,96},{24,120},{48,144},{72,168},{96,192},{120,216},{144,240},{16... | collective-permute-start | bytes 1572872 | tf_op jit(solution)/shard_map/while/body/eval_jaxpr/ppermute | solution.py:15
  140.5 12.0 %collective-permute-start.2 = (bf16[2,512,128]{2,1,0:T(8,128)(2,1)S(1)}, bf16[2,512,128]{2,1,0:T(8,128)(2,1)S(1)}, u32[]{:S(2)}, u32[]{:S(2)}) collective-permute-start(bf16[2,512,128]{2,1,0:T(8,128)(2,1)S(1)} %copy.65), channel_id=1, source_target_pairs={{0,96},{24,120},{48,144},{72,168},{96,192},{120,216},{144,240},{16... | collective-permute-start | bytes 786440 | tf_op jit(solution)/shard_map/while/body/eval_jaxpr/ppermute | solution.py:15
  160.4 14.6 %collective-permute-start.1 = (f32[2,512,128]{2,1,0:T(8,128)S(1)}, f32[2,512,128]{2,1,0:T(8,128)}, u32[]{:S(2)}, u32[]{:S(2)}) collective-permute-start(f32[2,512,128]{2,1,0:T(8,128)S(1)} %get-tuple-element.1331), channel_id=1, source_target_pairs={{0,96},{24,120},{48,144},{72,168},{96,192},{120,216},{144,240},{16... | collective-permute-start | bytes 1572872 | tf_op jit(solution)/shard_map/while/body/eval_jaxpr/ppermute | solution.py:15
  162.4 15.4 %collective-permute-start.2 = (bf16[2,512,128]{2,1,0:T(8,128)(2,1)S(1)}, bf16[2,512,128]{2,1,0:T(8,128)(2,1)S(1)}, u32[]{:S(2)}, u32[]{:S(2)}) collective-permute-start(bf16[2,512,128]{2,1,0:T(8,128)(2,1)S(1)} %copy.65), channel_id=1, source_target_pairs={{0,96},{24,120},{48,144},{72,168},{96,192},{120,216},{144,240},{16... | collective-permute-start | bytes 786440 | tf_op jit(solution)/shard_map/while/body/eval_jaxpr/ppermute | solution.py:15
  185.7 15.7 %collective-permute-start.1 = (f32[2,512,128]{2,1,0:T(8,128)S(1)}, f32[2,512,128]{2,1,0:T(8,128)}, u32[]{:S(2)}, u32[]{:S(2)}) collective-permute-start(f32[2,512,128]{2,1,0:T(8,128)S(1)} %get-tuple-element.1331), channel_id=1, source_target_pairs={{0,96},{24,120},{48,144},{72,168},{96,192},{120,216},{144,240},{16... | collective-permute-start | bytes 1572872 | tf_op jit(solution)/shard_map/while/body/eval_jaxpr/ppermute | solution.py:15
  187.6 16.5 %collective-permute-start.2 = (bf16[2,512,128]{2,1,0:T(8,128)(2,1)S(1)}, bf16[2,512,128]{2,1,0:T(8,128)(2,1)S(1)}, u32[]{:S(2)}, u32[]{:S(2)}) collective-permute-start(bf16[2,512,128]{2,1,0:T(8,128)(2,1)S(1)} %copy.65), channel_id=1, source_target_pairs={{0,96},{24,120},{48,144},{72,168},{96,192},{120,216},{144,240},{16... | collective-permute-start | bytes 786440 | tf_op jit(solution)/shard_map/while/body/eval_jaxpr/ppermute | solution.py:15
  212.0 16.9 %collective-permute-start.1 = (f32[2,512,128]{2,1,0:T(8,128)S(1)}, f32[2,512,128]{2,1,0:T(8,128)}, u32[]{:S(2)}, u32[]{:S(2)}) collective-permute-start(f32[2,512,128]{2,1,0:T(8,128)S(1)} %get-tuple-element.1331), channel_id=1, source_target_pairs={{0,96},{24,120},{48,144},{72,168},{96,192},{120,216},{144,240},{16... | collective-permute-start | bytes 1572872 | tf_op jit(solution)/shard_map/while/body/eval_jaxpr/ppermute | solution.py:15
  214.0 17.6 %collective-permute-start.2 = (bf16[2,512,128]{2,1,0:T(8,128)(2,1)S(1)}, bf16[2,512,128]{2,1,0:T(8,128)(2,1)S(1)}, u32[]{:S(2)}, u32[]{:S(2)}) collective-permute-start(bf16[2,512,128]{2,1,0:T(8,128)(2,1)S(1)} %copy.65), channel_id=1, source_target_pairs={{0,96},{24,120},{48,144},{72,168},{96,192},{120,216},{144,240},{16... | collective-permute-start | bytes 786440 | tf_op jit(solution)/shard_map/while/body/eval_jaxpr/ppermute | solution.py:15
  239.5 17.1 %collective-permute-start.1 = (f32[2,512,128]{2,1,0:T(8,128)S(1)}, f32[2,512,128]{2,1,0:T(8,128)}, u32[]{:S(2)}, u32[]{:S(2)}) collective-permute-start(f32[2,512,128]{2,1,0:T(8,128)S(1)} %get-tuple-element.1331), channel_id=1, source_target_pairs={{0,96},{24,120},{48,144},{72,168},{96,192},{120,216},{144,240},{16... | collective-permute-start | bytes 1572872 | tf_op jit(solution)/shard_map/while/body/eval_jaxpr/ppermute | solution.py:15
  241.4 18.7 %collective-permute-start.2 = (bf16[2,512,128]{2,1,0:T(8,128)(2,1)S(1)}, bf16[2,512,128]{2,1,0:T(8,128)(2,1)S(1)}, u32[]{:S(2)}, u32[]{:S(2)}) collective-permute-start(bf16[2,512,128]{2,1,0:T(8,128)(2,1)S(1)} %copy.65), channel_id=1, source_target_pairs={{0,96},{24,120},{48,144},{72,168},{96,192},{120,216},{144,240},{16... | collective-permute-start | bytes 786440 | tf_op jit(solution)/shard_map/while/body/eval_jaxpr/ppermute | solution.py:15
  268.0 17.0 %collective-permute-start.1 = (f32[2,512,128]{2,1,0:T(8,128)S(1)}, f32[2,512,128]{2,1,0:T(8,128)}, u32[]{:S(2)}, u32[]{:S(2)}) collective-permute-start(f32[2,512,128]{2,1,0:T(8,128)S(1)} %get-tuple-element.1331), channel_id=1, source_target_pairs={{0,96},{24,120},{48,144},{72,168},{96,192},{120,216},{144,240},{16... | collective-permute-start | bytes 1572872 | tf_op jit(solution)/shard_map/while/body/eval_jaxpr/ppermute | solution.py:15
  269.9 19.7 %collective-permute-start.2 = (bf16[2,512,128]{2,1,0:T(8,128)(2,1)S(1)}, bf16[2,512,128]{2,1,0:T(8,128)(2,1)S(1)}, u32[]{:S(2)}, u32[]{:S(2)}) collective-permute-start(bf16[2,512,128]{2,1,0:T(8,128)(2,1)S(1)} %copy.65), channel_id=1, source_target_pairs={{0,96},{24,120},{48,144},{72,168},{96,192},{120,216},{144,240},{16... | collective-permute-start | bytes 786440 | tf_op jit(solution)/shard_map/while/body/eval_jaxpr/ppermute | solution.py:15
  297.6 16.7 %collective-permute-start.1 = (f32[2,512,128]{2,1,0:T(8,128)S(1)}, f32[2,512,128]{2,1,0:T(8,128)}, u32[]{:S(2)}, u32[]{:S(2)}) collective-permute-start(f32[2,512,128]{2,1,0:T(8,128)S(1)} %get-tuple-element.1331), channel_id=1, source_target_pairs={{0,96},{24,120},{48,144},{72,168},{96,192},{120,216},{144,240},{16... | collective-permute-start | bytes 1572872 | tf_op jit(solution)/shard_map/while/body/eval_jaxpr/ppermute | solution.py:15
  299.5 20.3 %collective-permute-start.2 = (bf16[2,512,128]{2,1,0:T(8,128)(2,1)S(1)}, bf16[2,512,128]{2,1,0:T(8,128)(2,1)S(1)}, u32[]{:S(2)}, u32[]{:S(2)}) collective-permute-start(bf16[2,512,128]{2,1,0:T(8,128)(2,1)S(1)} %copy.65), channel_id=1, source_target_pairs={{0,96},{24,120},{48,144},{72,168},{96,192},{120,216},{144,240},{16... | collective-permute-start | bytes 786440 | tf_op jit(solution)/shard_map/while/body/eval_jaxpr/ppermute | solution.py:15
  325.3 13.3 %collective-permute-start.3 = (f32[2,512,128]{2,1,0:T(8,128)S(1)}, f32[2,512,128]{2,1,0:T(8,128)S(1)}, u32[]{:S(2)}, u32[]{:S(2)}) collective-permute-start(f32[2,512,128]{2,1,0:T(8,128)S(1)} %get-tuple-element.1006), channel_id=1, source_target_pairs={{0,96},{24,120},{48,144},{72,168},{96,192},{120,216},{144,240},{16... | collective-permute-start | bytes 1572872 | tf_op jit(solution)/shard_map/ppermute | solution.py:15
  (1 other events, 2.7 us)
where the time goes:
time: 539 us; the launch traced here: 532 us
  blocking collectives  190 us (35%)
  waiting for transfers between devices  140 us (26%)
  local copies, waits for them, and re-layouts  54.2 us (10%)
  matrix products  48.4 us (9%)
  starting transfers between devices  45 us (8%)
  other arithmetic  41 us (8%)
  loops' own time  11 us (2%)
    psum x1, blocking collectives, per_device(): summed = lax.psum(spread, 'head')  190 us
    ppermute x22, waiting for transfers between devices, shifted(): return lax.ppermute(value, axis, pairs)  140 us
    ppermute x22, starting transfers between devices, shifted(): return lax.ppermute(value, axis, pairs)  45 us
    dot_general x32, matrix products, contract_last(): lax.dot_general(left, right, (((1,), (1,)), ((), ())), preferred_element_...  30.5 us
    dot_general x16, matrix products, contract_first(): lax.dot_general(left, right, (((0,), (0,)), ((), ())), preferred_element_...  12 us
    gather x32, local copies, waits for them, and re-layouts, hop_mask(): entries = mask_table[query_ids, key_ids]  11.9 us
    broadcast_in_dim x16, local copies, waits for them, and re-layouts, hop_mask(): allowed = jnp.broadcast_to(allowed, (QB_DEV, BLK, local_heads, QB_DEV, BLK))  10.8 us
  transfers between devices with their start and end apart: 22, of which 22 were waited for; matrix products, arithmetic and copies ran while one was open for 4% of the time, Pallas kernels for 0%

commit v1 on v0

v1 whole, which is shorter than its diff:
```python
import functools
import math

import jax
import jax.numpy as jnp
from jax import lax
from jax.experimental import pallas as pl
from jax.experimental.pallas import tpu as pltpu
from jax.sharding import PartitionSpec as P

GROUP = 16
BLK = 128
SEQS = 4
QB_DEV = 4
CORES = 2
X = 4
NEG = -1e30
VMEM_BYTES = 60 * 1024 * 1024
MESH = pl.DeviceIdType.MESH


class Place:
    def __init__(self, members, planes):
        self.members = members
        self.planes = planes
        ctx = lax.axis_index("ctx")
        head = lax.axis_index("head")
        self.seq = ctx % SEQS
        self.y = ctx // SEQS
        self.core = head % CORES
        self.x = head // CORES % X
        self.z = head // (CORES * X)
        self.ctx = ctx
        self.head = head

    def member(self, steps):
        return (self.y + steps + self.members) % self.members

    def along_y(self, steps):
        return (self.member(steps) * SEQS + self.seq, self.head)

    def head_id(self, z, x, core):
        return (self.ctx, (z * X + x) * CORES + core)

    def sibling(self):
        return self.head_id(self.z, self.x, 1 - self.core)


def meet(partners):
    barrier = pltpu.get_barrier_semaphore()
    for partner in partners:
        pl.semaphore_signal(barrier, inc=1, device_id=partner, device_id_type=MESH)
    pl.semaphore_wait(barrier, len(partners))


def remote(src, dst, send_sem, recv_sem, target):
    return pltpu.make_async_remote_copy(
        src_ref=src,
        dst_ref=dst,
        send_sem=send_sem,
        recv_sem=recv_sem,
        device_id=target,
        device_id_type=MESH,
    )


def gather_kernel(members, planes, kv_per_plane, k_ref, v_ref, kg_ref, vg_ref, own_sem,
                  send_sem, recv_sem, side_send, side_recv):
    place = Place(members, planes)
    half_way = members // 2
    rows = k_ref.shape[1]
    part = rows // CORES
    kv = place.z * kv_per_plane + place.x * kv_per_plane // X
    mine = pl.ds(place.core * part, part)
    other = pl.ds((1 - place.core) * part, part)
    pairs = ((k_ref, kg_ref), (v_ref, vg_ref))
    own = [
        pltpu.make_async_copy(src.at[kv], dst.at[place.y], own_sem.at[index])
        for index, (src, dst) in enumerate(pairs)
    ]
    meet([place.along_y(1), place.along_y(-1), place.sibling()])
    started = []
    chains = []
    for tensor in range(2):
        for way, sign in enumerate((1, -1)):
            hops = half_way if tensor == way else half_way - 1
            chains.append((tensor, way, sign, hops))

    def ring_copy(tensor, way, sign, step):
        src_in, dst = pairs[tensor]
        at = dst.at[place.member(-sign * step), mine]
        src = src_in.at[kv, mine] if step == 0 else at
        return remote(
            src, at, send_sem.at[tensor, way, step], recv_sem.at[tensor, way, step], place.along_y(sign)
        )

    def arrival(tensor, way, sign, step):
        at = pairs[tensor][1].at[place.member(-sign * (step + 1)), mine]
        return remote(
            at, at, send_sem.at[tensor, way, step], recv_sem.at[tensor, way, step], place.along_y(sign)
        )

    def side_copy(tensor, way, sign, step, rows_at):
        at = pairs[tensor][1].at[place.member(-sign * (step + 1)), rows_at]
        return remote(
            at, at, side_send.at[tensor, way, step], side_recv.at[tensor, way, step], place.sibling()
        )

    for chain in chains:
        copy = ring_copy(*chain[:3], 0)
        copy.start()
        started.append(copy)
    for copy in own:
        copy.start()
    for step in range(half_way):
        for tensor, way, sign, hops in chains:
            if step >= hops:
                continue
            arrival(tensor, way, sign, step).wait_recv()
            if step + 1 < hops:
                copy = ring_copy(tensor, way, sign, step + 1)
                copy.start()
                started.append(copy)
            copy = side_copy(tensor, way, sign, step, mine)
            copy.start()
            started.append(copy)
    for tensor, way, sign, hops in chains:
        for step in range(hops):
            side_copy(tensor, way, sign, step, other).wait_recv()
    for copy in started:
        copy.wait_send()
    for copy in own:
        copy.wait()


def gather(members, planes, keys, values):
    kv_count, rows, depth = keys.shape
    out = jax.ShapeDtypeStruct((members, rows, depth), keys.dtype)
    hops = members // 2
    return pl.pallas_call(
        functools.partial(gather_kernel, members, planes, kv_count // planes),
        out_shape=(out, out),
        in_specs=[pl.BlockSpec(memory_space=pl.ANY)] * 2,
        out_specs=[pl.BlockSpec(memory_space=pl.ANY)] * 2,
        scratch_shapes=[pltpu.SemaphoreType.DMA((2,))]
        + [pltpu.SemaphoreType.DMA((2, 2, hops))] * 4,
        compiler_params=pltpu.CompilerParams(collective_id=0, has_side_effects=True),
        name="gather_keys",
    )(keys, values)


def dot(left, right):
    return jnp.dot(left, right, preferred_element_type=jnp.float32)


def dot_first(left, right):
    return lax.dot_general(left, right, (((0,), (0,)), ((), ())), preferred_element_type=jnp.float32)


def grad_kernel(members, order_ref, mask_ref, q_ref, g_ref, k_ref, v_ref, dq_ref, dkv_ref,
                list_ref, score_ref, dprob_ref, acc_ref, dq_acc, qt_ref, gt_ref):
    ctx = lax.axis_index("ctx")
    seq = ctx % SEQS
    member = ctx // SEQS
    depth = q_ref.shape[1]
    rows = q_ref.shape[0] // QB_DEV
    heads = rows // BLK
    slots = members * QB_DEV
    scale = depth ** -0.5
    scale2 = scale * math.log2(math.e)
    acc_ref[...] = jnp.zeros_like(acc_ref)

    def pair(ref, first, second):
        return jnp.concatenate([ref[first], ref[second]], axis=0)

    def fold(value, op):
        return op(value.reshape(value.shape[0] // 8, 8, rows), axis=0)

    def spread(value, like):
        count = like.shape[0]
        return jnp.broadcast_to(value[None], (count // 8, 8, rows)).reshape(count, rows)

    def query_block(index, carry):
        own = member * QB_DEV + index
        query_pos = order_ref[seq, own]

        def list_slot(slot, count):
            key_pos = order_ref[seq, slot]
            list_ref[count] = slot
            seen = jnp.logical_and(key_pos < query_pos, mask_ref[seq, query_pos, key_pos] == 1)
            return count + seen.astype(jnp.int32)

        count = lax.fori_loop(0, slots, list_slot, 0, unroll=8)
        pairs = count // 2
        odd = count % 2 == 1
        at = pl.ds(pl.multiple_of(index * rows, rows), rows)
        qt_ref[...] = q_ref[at, :].T
        gt_ref[...] = g_ref[at, :].T

        def place_of(number):
            return pl.ds(pl.multiple_of(BLK + number * 2 * BLK, BLK), 2 * BLK)

        tail_at = pl.ds(pl.multiple_of(BLK + pairs * 2 * BLK, BLK), BLK)

        def over(diagonal, two, one, init):
            state = diagonal(init)

            def body(number, state):
                first, second = list_ref[2 * number], list_ref[2 * number + 1]
                return two(first, second, place_of(number), state)

            state = lax.fori_loop(0, pairs, body, state)
            return lax.cond(odd, lambda kept: one(list_ref[2 * pairs], tail_at, kept), lambda kept: kept, state)

        first_at = pl.ds(0, BLK)

        def score_diagonal(maxima):
            score = dot(k_ref[own], qt_ref[...])
            key_token = lax.broadcasted_iota(jnp.int32, (BLK, rows), 0)
            query_token = lax.broadcasted_iota(jnp.int32, (BLK, rows), 1) // heads
            score = jnp.where(key_token <= query_token, score, NEG)
            score_ref[first_at, :] = score
            return jnp.maximum(maxima, fold(score, jnp.max))

        def score_two(first, second, where, maxima):
            score = dot(pair(k_ref, first, second), qt_ref[...])
            score_ref[where, :] = score
            return jnp.maximum(maxima, fold(score, jnp.max))

        def score_one(slot, where, maxima):
            score = dot(k_ref[slot], qt_ref[...])
            score_ref[where, :] = score
            return jnp.maximum(maxima, fold(score, jnp.max))

        maxima = over(score_diagonal, score_two, score_one, jnp.full((8, rows), NEG, jnp.float32))
        top = jnp.broadcast_to(jnp.max(maxima, axis=0, keepdims=True), (8, rows)) * scale2

        def weigh(values, where, state):
            totals, weighted = state
            dprob = dot(values, gt_ref[...])
            score = score_ref[where, :]
            exp_part = jnp.exp2(score * scale2 - spread(top, score))
            score_ref[where, :] = exp_part
            dprob_ref[where, :] = dprob
            return totals + fold(exp_part, jnp.sum), weighted + fold(exp_part * dprob, jnp.sum)

        zero = jnp.zeros((8, rows), jnp.float32)
        totals, weighted = over(
            lambda state: weigh(v_ref[own], first_at, state),
            lambda first, second, where, state: weigh(pair(v_ref, first, second), where, state),
            lambda slot, where, state: weigh(v_ref[slot], where, state),
            (zero, zero),
        )
        total = jnp.sum(totals, axis=0, keepdims=True)
        inverse = 1.0 / total
        delta = jnp.broadcast_to(jnp.sum(weighted, axis=0, keepdims=True) * inverse, (8, rows))
        inverse = jnp.broadcast_to(inverse, (8, rows))

        def grads(where):
            exp_part = score_ref[where, :]
            prob = exp_part * spread(inverse, exp_part)
            dscore = prob * (dprob_ref[where, :] - spread(delta, exp_part))
            return prob.astype(jnp.bfloat16), dscore.astype(jnp.bfloat16)

        def grad_one(slot, where, first=False):
            prob, dscore = grads(where)
            acc_ref[0, slot] += dot(dscore, q_ref[at, :])
            acc_ref[1, slot] += dot(prob, g_ref[at, :])
            add = dot_first(dscore, k_ref[slot])
            dq_acc[...] = add if first else dq_acc[...] + add

        def grad_two(first, second, where):
            prob, dscore = grads(where)
            key_add = dot(dscore, q_ref[at, :])
            value_add = dot(prob, g_ref[at, :])
            acc_ref[0, first] += key_add[:BLK]
            acc_ref[0, second] += key_add[BLK:]
            acc_ref[1, first] += value_add[:BLK]
            acc_ref[1, second] += value_add[BLK:]
            dq_acc[...] += dot_first(dscore, pair(k_ref, first, second))

        grad_one(own, first_at, True)

        def grad_body(number, kept):
            grad_two(list_ref[2 * number], list_ref[2 * number + 1], place_of(number))
            return kept

        lax.fori_loop(0, pairs, grad_body, 0)

        @pl.when(odd)
        def _():
            grad_one(list_ref[2 * pairs], tail_at)

        dq_ref[at, :] = (dq_acc[...] * scale).astype(dq_ref.dtype)
        return carry

    lax.fori_loop(0, QB_DEV, query_block, 0)
    dkv_ref[0] = (acc_ref[0] * scale).astype(dkv_ref.dtype)
    dkv_ref[1] = acc_ref[1].astype(dkv_ref.dtype)


def local_grads(members, block_pos, block_mask, query_rows, grad_rows, keys, values):
    row_total, depth = query_rows.shape
    slots = members * QB_DEV
    rows = row_total // QB_DEV
    smem = pl.BlockSpec(memory_space=pltpu.SMEM)
    vmem = pl.BlockSpec(memory_space=pltpu.VMEM)
    return pl.pallas_call(
        functools.partial(grad_kernel, members),
        out_shape=(
            jax.ShapeDtypeStruct((row_total, depth), jnp.bfloat16),
            jax.ShapeDtypeStruct((2, slots, BLK, depth), jnp.bfloat16),
        ),
        in_specs=[smem, smem, vmem, vmem, vmem, vmem],
        out_specs=(vmem, vmem),
        scratch_shapes=[
            pltpu.SMEM((slots + 1,), jnp.int32),
            pltpu.VMEM(((slots + 2) * BLK, rows), jnp.float32),
            pltpu.VMEM(((slots + 2) * BLK, rows), jnp.float32),
            pltpu.VMEM((2, slots, BLK, depth), jnp.float32),
            pltpu.VMEM((rows, depth), jnp.float32),
            pltpu.VMEM((depth, rows), jnp.bfloat16),
            pltpu.VMEM((depth, rows), jnp.bfloat16),
        ],
        compiler_params=pltpu.CompilerParams(vmem_limit_bytes=VMEM_BYTES),
        name="local_grads",
    )(block_pos, block_mask, query_rows, grad_rows,
      keys.reshape(slots, BLK, depth), values.reshape(slots, BLK, depth))


def reduce_kernel(members, planes, part_ref, out_ref, side, sums, landed, total, piece, swap,
                  side_send, side_recv, ring_send, ring_recv, pair_sem, own_sem,
                  z_send, z_recv, x_send, x_recv, twin_send, twin_recv):
    place = Place(members, planes)
    half_way = members // 2
    rows = part_ref.shape[2]
    half = rows // 2
    core = place.core
    pair_x = place.x + 1 - 2 * (place.x % 2)
    partner = place.head_id(place.z, pair_x, core)
    z_ids = [(place.z + step) % planes for step in range(1, planes)]
    x_ids = [(place.x + step) % X for step in range(1, X)]
    meet(
        [place.along_y(1), place.along_y(-1), place.sibling()]
        + [place.head_id(place.z, x, core) for x in x_ids]
        + [place.head_id(z, place.x, core) for z in z_ids]
    )
    started = []

    def start(copy):
        copy.start()
        started.append(copy)

    offsets = [half_way]
    for steps in range(half_way - 1, 0, -1):
        offsets += [steps, -steps]
    offsets.append(0)

    def side_copy(steps):
        at = place.member(steps)
        slot = offsets.index(steps)
        return remote(part_ref.at[1 - core, at], side.at[slot], side_send.at[slot], side_recv.at[slot], place.sibling())

    for steps in offsets:
        start(side_copy(steps))

    def base(steps, which):
        slot = offsets.index(steps)
        at = place.member(steps)
        rows_at = pl.ds(which * half, half)
        return (part_ref[core, at, rows_at, :].astype(jnp.float32)
                + side[slot, rows_at, :].astype(jnp.float32))

    def ring_copy(way, step, which):
        return remote(
            sums.at[way, step, which],
            landed.at[way, step, which],
            ring_send.at[way, step, which],
            ring_recv.at[way, step, which],
            place.along_y(1 - 2 * way),
        )

    def begins(way, which):
        return 0 if way == which else 1

    def ring_step(way, step, which):
        sign = 1 - 2 * way
        steps = sign * (half_way - step)
        value = base(half_way if step == 0 else steps, which)
        if step > begins(way, which):
            ring_copy(way, step - 1, which).wait_recv()
            value = value + landed[way, step - 1, which].astype(jnp.float32)
        sums[way, step, which] = value.astype(sums.dtype)
        start(ring_copy(way, step, which))

    side_copy(half_way).wait_recv()
    ring_step(0, 0, 0)
    ring_step(1, 0, 1)
    for step in range(1, half_way):
        order = ((0, 1), (1, 0), (0, 0), (1, 1)) if step == 1 else ((0, 0), (1, 1), (0, 1), (1, 0))
        waited = set()
        for way, which in order:
            steps = (1 - 2 * way) * (half_way - step)
            if steps not in waited:
                side_copy(steps).wait_recv()
                waited.add(steps)
            ring_step(way, step, which)
    side_copy(0).wait_recv()
    for which in range(2):
        value = base(0, which)
        for way in range(2):
            ring_copy(way, half_way - 1, which).wait_recv()
            value = value + landed[way, half_way - 1, which].astype(jnp.float32)
        total[which] = value
    keep = place.x % 2
    swap[0] = total[1 - keep].astype(swap.dtype)
    swap_copy = remote(swap.at[0], swap.at[1], pair_sem.at[0], pair_sem.at[1], partner)
    start(swap_copy)
    swap_copy.wait_recv()
    piece[...] = (total[keep] + swap[1].astype(jnp.float32)).astype(piece.dtype)

    def spot(tensor, z, x):
        return out_ref.at[tensor, z * (X // 2) + x // 2, pl.ds(x % 2 * half, half)]

    here = spot(core, place.z, place.x)
    for number, z in enumerate(z_ids):
        start(remote(piece, here, z_send.at[number], z_recv.at[number], place.head_id(z, place.x, core)))
    for number, x in enumerate(x_ids):
        start(remote(piece, here, x_send.at[0, number], x_recv.at[0, number], place.head_id(place.z, x, core)))
    start(remote(piece, here, twin_send.at[0, 0], twin_recv.at[0, 0], place.sibling()))
    own = pltpu.make_async_copy(piece, here, own_sem)
    own.start()

    def landing(sem_send, sem_recv, spot_at):
        remote(spot_at, spot_at, sem_send, sem_recv, place.sibling()).wait_recv()

    for number in range(planes - 1):
        z = (place.z - number - 1 + planes) % planes
        spot_at = spot(core, z, place.x)
        landing(z_send.at[number], z_recv.at[number], spot_at)
        for index, x in enumerate(x_ids):
            start(remote(spot_at, spot_at, x_send.at[number + 1, index], x_recv.at[number + 1, index],
                         place.head_id(place.z, x, core)))
        start(remote(spot_at, spot_at, twin_send.at[number + 1, 0], twin_recv.at[number + 1, 0], place.sibling()))
    for number in range(planes):
        z = (place.z - number + planes) % planes
        for index in range(X - 1):
            x = (place.x - index - 1 + X) % X
            spot_at = spot(core, z, x)
            landing(x_send.at[number, index], x_recv.at[number, index], spot_at)
            start(remote(spot_at, spot_at, twin_send.at[number, index + 1], twin_recv.at[number, index + 1],
                         place.sibling()))
    for number in range(planes):
        z = (place.z - number + planes) % planes
        for index in range(X):
            x = (place.x - index + X) % X
            landing(twin_send.at[number, index], twin_recv.at[number, index], spot(1 - core, z, x))
    own.wait()
    for copy in started:
        copy.wait_send()


def reduce_sums(members, planes, kv_count, partial_sums):
    _, slots, _, depth = partial_sums.shape
    rows = slots // members * BLK
    half = rows // 2
    half_way = members // 2
    dma = pltpu.SemaphoreType.DMA
    low = jnp.bfloat16
    return pl.pallas_call(
        functools.partial(reduce_kernel, members, planes),
        out_shape=jax.ShapeDtypeStruct((2, kv_count, rows, depth), low),
        in_specs=[pl.BlockSpec(memory_space=pltpu.VMEM)],
        out_specs=pl.BlockSpec(memory_space=pl.ANY),
        scratch_shapes=[
            pltpu.VMEM((members, rows, depth), low),
            pltpu.VMEM((2, half_way, 2, half, depth), low),
            pltpu.VMEM((2, half_way, 2, half, depth), low),
            pltpu.VMEM((2, half, depth), jnp.float32),
            pltpu.VMEM((half, depth), low),
            pltpu.VMEM((2, half, depth), low),
            dma((members,)),
            dma((members,)),
            dma((2, half_way, 2)),
            dma((2, half_way, 2)),
            dma((2,)),
            dma,
            dma((max(planes - 1, 1),)),
            dma((max(planes - 1, 1),)),
            dma((planes, X - 1)),
            dma((planes, X - 1)),
            dma((planes, X)),
            dma((planes, X)),
        ],
        compiler_params=pltpu.CompilerParams(
            collective_id=1, has_side_effects=True, vmem_limit_bytes=VMEM_BYTES
        ),
        name="reduce_sums",
    )(partial_sums.reshape(2, members, rows, depth))


def per_device(queries, keys, values, d_out, block_pos, block_mask):
    members = lax.axis_size("ctx") // SEQS
    planes = lax.axis_size("head") // (CORES * X)
    tokens, heads, depth = queries.shape
    kv_count = keys.shape[1]
    key_all, value_all = gather(
        members, planes, jnp.transpose(keys, (1, 0, 2)), jnp.transpose(values, (1, 0, 2))
    )
    d_queries, partial_sums = local_grads(
        members,
        block_pos,
        block_mask,
        queries.reshape(tokens * heads, depth),
        d_out.reshape(tokens * heads, depth),
        key_all,
        value_all,
    )
    summed = reduce_sums(members, planes, kv_count, partial_sums)
    return (
        d_queries.reshape(tokens, heads, depth),
        jnp.transpose(summed[0], (1, 0, 2)),
        jnp.transpose(summed[1], (1, 0, 2)),
    )


def solution(mesh):
    placed = (
        P("ctx", "head", None),
        P("ctx", None, None),
        P("ctx", None, None),
        P("ctx", "head", None),
        P(),
        P(),
    )
    return jax.shard_map(
        per_device,
        mesh=mesh,
        in_specs=placed,
        out_specs=(P("ctx", "head", None), P("ctx", None, None), P("ctx", None, None)),
        check_vma=False,
    )
```

time: 539 us -> 105 us (0.19); the launches traced: 532 us -> 105 us
  blocking collectives: 190 us -> 0 us
  waiting for transfers between devices: 140 us -> 0 us
  Pallas kernels: 0 us -> 101 us
  local copies, waits for them, and re-layouts: 54.2 us -> 2.61 us
  matrix products: 48.4 us -> 0 us
  starting transfers between devices: 45 us -> 0 us
  other arithmetic: 41 us -> 0 us
  loops' own time: 11 us -> 0 us
    psum x1 -> x0, blocking collectives: 190 us -> none  [per_device(): summed = lax.psum(spread, 'head')]
    ppermute x22 -> x0, waiting for transfers between devices: 140 us -> none  [shifted(): return lax.ppermute(value, axis, pairs)]
    pallas_call x0 -> x3, Pallas kernels: none -> 101 us  [the longest x1 57.1 us: reduce_sums(): pl.pallas_call(functools.partial(reduce_kernel, members, planes), out_sha...]
    dot_general x56 -> x0, matrix products: 48.4 us -> none  [the longest x32 30.5 us: contract_last(): lax.dot_general(left, right, (((1,), (1,)), ((), ())), preferred_element_...]
    ppermute x22 -> x0, starting transfers between devices: 45 us -> none  [shifted(): return lax.ppermute(value, axis, pairs)]
    gather x32 -> x0, local copies, waits for them, and re-layouts: 11.9 us -> none  [hop_mask(): entries = mask_table[query_ids, key_ids]]
    another operation x18 -> x0, loops' own time: 11 us -> none  [the longest x1 4.96 us: per_device(): lax.fori_loop(0, cycle_members - 1, one_way, (stats, own_pair, kept_pairs))]
    broadcast_in_dim x18 -> x0, local copies, waits for them, and re-layouts: 10.9 us -> none  [the longest x16 10.8 us: hop_mask(): allowed = jnp.broadcast_to(allowed, (QB_DEV, BLK, local_heads, QB_DEV, BLK))]
  transfers between devices with their start and end apart: 22 -> 0, of which waited for: 22 -> 0; matrix products, arithmetic and copies ran while one was open for 4% -> 0% of each run, Pallas kernels for 0% -> 0%
where the time goes in v1:
time: 105 us
  Pallas kernels  101 us (96%)
  local copies, waits for them, and re-layouts  2.61 us (2%)
    pallas_call x1, Pallas kernels, reduce_sums(): pl.pallas_call(functools.partial(reduce_kernel, members, planes), out_sha...  57.1 us
    pallas_call x1, Pallas kernels, gather(): pl.pallas_call(functools.partial(gather_kernel, members, planes, kv_count...  30.6 us
    pallas_call x1, Pallas kernels, local_grads(): pl.pallas_call(functools.partial(grad_kernel, members), out_shape=(jax.Sh...  13.7 us
    transpose x1, local copies, waits for them, and re-layouts, per_device(): jnp.transpose(summed[1], (1, 0, 2))  2.61 us

profile of v1, /device:TPU:1, one launch (start us, length us, event | category | flops | bytes accessed | tf_op | source)
XLA Modules:
  0.0 104.7 jit_solution(18116073878751372369)
XLA Ops:
  0.6 30.6 %gather_keys.1 = (bf16[8,512,128]{2,1,0:T(8,128)(2,1)}, bf16[8,512,128]{2,1,0:T(8,128)(2,1)}) custom-call(bf16[6,512,128]{2,1,0:T(8,128)(2,1)} %bitcast.19, bf16[6,512,128]{2,1,0:T(8,128)(2,1)} %bitcast.20), custom_call_target="tpu_custom_call" | custom-call | tf_op jit(solution)/shard_map/gather_keys/pallas_call | solution.py:140
  31.3 13.7 %local_grads.1 = (bf16[2048,128]{1,0:T(8,128)(2,1)}, bf16[2,32,128,128]{3,2,1,0:T(8,128)(2,1)}) custom-call(s32[4,32]{1,0:T(4,128)} %order_ref.1, s32[4,32,32]{2,1,0:T(8,128)} %mask_ref.1, bf16[2048,128]{1,0:T(8,128)(2,1)} %bitcast.21, bf16[2048,128]{1,0:T(8,128)(2,1)} %bitcast.22, bf16[32,128,128]{2,1,0:T(8,128)(2,1)} %bitcast.17, ...), custom_call_target="tpu_custom_call" | custom-call | tf_op jit(solution)/shard_map/local_grads/pallas_call | solution.py:308
  45.0 57.1 %reduce_sums.1 = bf16[2,6,512,128]{3,2,1,0:T(8,128)(2,1)} custom-call(bf16[2,8,512,128]{3,2,1,0:T(8,128)(2,1)} %bitcast.16), custom_call_target="tpu_custom_call" | custom-call | tf_op jit(solution)/shard_map/reduce_sums/pallas_call | solution.py:470
  102.1 2.6 %slice_bitcast_fusion = (bf16[512,6,128]{2,0,1:T(8,128)(2,1)}, bf16[512,6,128]{2,0,1:T(8,128)(2,1)}) fusion(bf16[2,6,512,128]{3,2,1,0:T(8,128)(2,1)} %reduce_sums.1), kind=kLoop, calls=%fused_computation | loop fusion | bytes 3145728 | tf_op jit(solution)/shard_map/transpose | solution.py:523

commit v2 on v1

v2 whole, which is shorter than its diff:
```python
import functools
import math

import jax
import jax.numpy as jnp
from jax import lax
from jax.experimental import pallas as pl
from jax.experimental.pallas import tpu as pltpu
from jax.sharding import PartitionSpec as P

GROUP = 16
BLK = 128
SEQS = 4
QB_DEV = 4
CORES = 2
X = 4
NEG = -1e30
WIDE = 8
UNROLL = 32
VMEM_BYTES = 44 * 1024 * 1024
SMALL_VMEM_BYTES = 16 * 1024 * 1024
MESH = pl.DeviceIdType.MESH


class Place:
    def __init__(self, members, planes):
        self.members = members
        self.planes = planes
        ctx = lax.axis_index("ctx")
        head = lax.axis_index("head")
        self.seq = ctx % SEQS
        self.y = ctx // SEQS
        self.core = head % CORES
        self.x = head // CORES % X
        self.z = head // (CORES * X)
        self.ctx = ctx
        self.head = head

    def member(self, steps):
        return (self.y + steps + self.members) % self.members

    def along_y(self, steps):
        return (self.member(steps) * SEQS + self.seq, self.head)

    def head_id(self, z, x, core):
        return (self.ctx, (z * X + x) * CORES + core)

    def sibling(self):
        return self.head_id(self.z, self.x, 1 - self.core)


def meet(partners):
    barrier = pltpu.get_barrier_semaphore()
    for partner in partners:
        pl.semaphore_signal(barrier, inc=1, device_id=partner, device_id_type=MESH)
    pl.semaphore_wait(barrier, len(partners))


def remote(src, dst, send_sem, recv_sem, target):
    return pltpu.make_async_remote_copy(
        src_ref=src,
        dst_ref=dst,
        send_sem=send_sem,
        recv_sem=recv_sem,
        device_id=target,
        device_id_type=MESH,
    )


def gather_kernel(members, planes, kv_per_plane, k_ref, v_ref, kg_ref, vg_ref, own_sem,
                  send_sem, recv_sem, side_send, side_recv):
    place = Place(members, planes)
    part = k_ref.shape[1] // CORES
    kv = place.z * kv_per_plane + place.x * kv_per_plane // X
    mine = pl.ds(place.core * part, part)
    other = pl.ds((1 - place.core) * part, part)
    pairs = ((k_ref, kg_ref), (v_ref, vg_ref))
    own = [
        pltpu.make_async_copy(src.at[kv], dst.at[place.y], own_sem.at[index])
        for index, (src, dst) in enumerate(pairs)
    ]
    meet([place.along_y(steps) for steps in (1, -1, 2, -2)] + [place.sibling()])
    started = []
    chains = [(tensor, way) for tensor in range(2) for way in range(2)]

    def start(copy):
        copy.start()
        started.append(copy)

    def send(tensor, way, origin, reach, steps):
        sign = 1 - 2 * way
        src_in, dst = pairs[tensor]
        at = dst.at[place.member(-sign * origin), mine]
        src = src_in.at[kv, mine] if origin == 0 else at
        start(remote(src, at, send_sem.at[tensor, way, reach - 1], recv_sem.at[tensor, way, reach - 1],
                     place.along_y(sign * steps)))

    def side_copy(tensor, way, reach, rows_at):
        at = pairs[tensor][1].at[place.member(-(1 - 2 * way) * reach), rows_at]
        return remote(at, at, side_send.at[tensor, way, reach - 1], side_recv.at[tensor, way, reach - 1],
                      place.sibling())

    def arrived(tensor, way, reach):
        at = pairs[tensor][1].at[place.member(-(1 - 2 * way) * reach), mine]
        remote(at, at, send_sem.at[tensor, way, reach - 1], recv_sem.at[tensor, way, reach - 1],
               place.sibling()).wait_recv()

    for tensor, way in chains:
        send(tensor, way, 0, 2, 2)
    for tensor, way in chains:
        send(tensor, way, 0, 1, 1)
    for copy in own:
        copy.start()
    for tensor, way in chains:
        arrived(tensor, way, 2)
        if tensor == way:
            send(tensor, way, 2, 4, 2)
        send(tensor, way, 2, 3, 1)
    steps = [(tensor, way, 2) for tensor, way in chains]
    for reach in (1, 3, 4):
        steps += [(tensor, way, reach) for tensor, way in chains if reach < 4 or tensor == way]
    for tensor, way, reach in steps:
        if reach != 2:
            arrived(tensor, way, reach)
        start(side_copy(tensor, way, reach, mine))
    for step in steps:
        side_copy(*step, other).wait_recv()
    for copy in started:
        copy.wait_send()
    for copy in own:
        copy.wait()


def gather(members, planes, keys, values):
    kv_count, rows, depth = keys.shape
    out = pltpu.VMEM((members, rows, depth), keys.dtype)
    return pl.pallas_call(
        functools.partial(gather_kernel, members, planes, kv_count // planes),
        out_shape=(out, out),
        in_specs=[pl.BlockSpec(memory_space=pl.ANY)] * 2,
        out_specs=[pl.BlockSpec(memory_space=pltpu.VMEM)] * 2,
        scratch_shapes=[pltpu.SemaphoreType.DMA((2,))]
        + [pltpu.SemaphoreType.DMA((2, 2, members // 2))] * 4,
        compiler_params=pltpu.CompilerParams(
            collective_id=0, has_side_effects=True, vmem_limit_bytes=SMALL_VMEM_BYTES
        ),
        name="gather_keys",
    )(keys, values)


def dot(left, right):
    return jnp.dot(left, right, preferred_element_type=jnp.float32)


def dot_first(left, right):
    return lax.dot_general(left, right, (((0,), (0,)), ((), ())), preferred_element_type=jnp.float32)


def grad_kernel(members, order_ref, mask_ref, q_ref, g_ref, k_ref, v_ref, dq_ref, dkv_ref,
                list_ref, exp_ref, dprob_ref, top_ref, acc_ref, dq_acc, qt_ref, gt_ref):
    ctx = lax.axis_index("ctx")
    seq = ctx % SEQS
    member = ctx // SEQS
    depth = q_ref.shape[1]
    rows = q_ref.shape[0] // QB_DEV
    heads = rows // BLK
    slots = members * QB_DEV
    scale = depth ** -0.5
    scale2 = scale * math.log2(math.e)
    acc_ref[...] = jnp.zeros_like(acc_ref)
    query_pos = [order_ref[seq, member * QB_DEV + index] for index in range(QB_DEV)]

    def list_slot(slot, counts):
        key_pos = order_ref[seq, slot]
        grown = []
        for index, count in enumerate(counts):
            list_ref[index, count] = slot
            seen = jnp.logical_and(key_pos < query_pos[index], mask_ref[seq, query_pos[index], key_pos] == 1)
            grown.append(count + seen.astype(jnp.int32))
        return tuple(grown)

    counts = lax.fori_loop(0, slots, list_slot, (jnp.int32(0),) * QB_DEV, unroll=UNROLL)
    for index, count in enumerate(counts):
        list_ref[index, slots + 1] = count

    def blocks(ref, picked):
        return jnp.concatenate([ref[slot] for slot in picked], axis=0) if len(picked) > 1 else ref[picked[0]]

    def fold(value, op):
        return op(value.reshape(value.shape[0] // 8, 8, rows), axis=0)

    def spread(value, count):
        return jnp.broadcast_to(value[None], (count // 8, 8, rows)).reshape(count, rows)

    def query_block(index, carry):
        own = member * QB_DEV + index
        count = list_ref[index, slots + 1]
        at = pl.ds(pl.multiple_of(index * rows, rows), rows)
        qt_ref[...] = q_ref[at, :].T
        gt_ref[...] = g_ref[at, :].T

        def part(start, size, body, state):
            picked = [list_ref[index, start + offset] for offset in range(size)]
            where = pl.ds(pl.multiple_of((start + 1) * BLK, BLK), size * BLK)
            return body(picked, where, start + 1, state)

        def over(body, state):
            state = lax.fori_loop(0, count // WIDE, lambda n, state: part(n * WIDE, WIDE, body, state), state)
            size = WIDE // 2
            while size:
                start = count // (2 * size) * (2 * size)
                state = lax.cond(
                    count // size % 2 == 1,
                    lambda state, start=start, size=size: part(start, size, body, state),
                    lambda state: state,
                    state,
                )
                size //= 2
            return state

        def weigh(picked, where, number, state, diagonal=False):
            maxima, totals, weighted = state
            score = dot(blocks(k_ref, picked), qt_ref[...])
            if diagonal:
                key_token = lax.broadcasted_iota(jnp.int32, (BLK, rows), 0)
                query_token = lax.broadcasted_iota(jnp.int32, (BLK, rows), 1) // heads
                score = jnp.where(key_token <= query_token, score, NEG)
            dprob = dot(blocks(v_ref, picked), gt_ref[...])
            new = jnp.maximum(maxima, fold(score, jnp.max))
            top = new * scale2
            factor = jnp.exp2(maxima * scale2 - top)
            exp_part = jnp.exp2(score * scale2 - spread(top, score.shape[0]))
            exp_ref[where, :] = exp_part
            dprob_ref[where, :] = dprob
            top_ref[number] = top
            return (
                new,
                totals * factor + fold(exp_part, jnp.sum),
                weighted * factor + fold(exp_part * dprob, jnp.sum),
            )

        zero = jnp.zeros((8, rows), jnp.float32)
        first_at = pl.ds(0, BLK)
        state = weigh([own], first_at, 0, (zero + NEG, zero, zero), True)
        maxima, totals, weighted = over(weigh, state)
        tops = maxima * scale2
        top = jnp.broadcast_to(jnp.max(tops, axis=0, keepdims=True), (8, rows))
        factor = jnp.exp2(tops - top)
        inverse = 1.0 / jnp.sum(totals * factor, axis=0, keepdims=True)
        delta = jnp.broadcast_to(jnp.sum(weighted * factor, axis=0, keepdims=True) * inverse, (8, rows))
        inverse = jnp.broadcast_to(inverse, (8, rows))

        def grads(picked, where, number, state, first=False):
            size = len(picked) * BLK
            share = jnp.exp2(top_ref[number] - top) * inverse
            prob = exp_ref[where, :] * spread(share, size)
            dscore = (prob * (dprob_ref[where, :] - spread(delta, size))).astype(jnp.bfloat16)
            key_add = dot(dscore, q_ref[at, :])
            value_add = dot(prob.astype(jnp.bfloat16), g_ref[at, :])
            for offset, slot in enumerate(picked):
                acc_ref[0, slot] += key_add[offset * BLK:(offset + 1) * BLK]
                acc_ref[1, slot] += value_add[offset * BLK:(offset + 1) * BLK]
            add = dot_first(dscore, blocks(k_ref, picked))
            dq_acc[...] = add if first else dq_acc[...] + add
            return state

        grads([own], first_at, 0, 0, True)
        over(grads, 0)
        dq_ref[at, :] = (dq_acc[...] * scale).astype(dq_ref.dtype)
        return carry

    lax.fori_loop(0, QB_DEV, query_block, 0)
    dkv_ref[0] = (acc_ref[0] * scale).astype(dkv_ref.dtype)
    dkv_ref[1] = acc_ref[1].astype(dkv_ref.dtype)


def local_grads(members, block_pos, block_mask, query_rows, grad_rows, keys, values):
    row_total, depth = query_rows.shape
    slots = members * QB_DEV
    rows = row_total // QB_DEV
    smem = pl.BlockSpec(memory_space=pltpu.SMEM)
    vmem = pl.BlockSpec(memory_space=pltpu.VMEM)
    return pl.pallas_call(
        functools.partial(grad_kernel, members),
        out_shape=(
            jax.ShapeDtypeStruct((row_total, depth), jnp.bfloat16),
            pltpu.VMEM((2, slots, BLK, depth), jnp.bfloat16),
        ),
        in_specs=[smem, smem, vmem, vmem, vmem, vmem],
        out_specs=(vmem, vmem),
        scratch_shapes=[
            pltpu.SMEM((QB_DEV, slots + 2), jnp.int32),
            pltpu.VMEM((slots * BLK, rows), jnp.float32),
            pltpu.VMEM((slots * BLK, rows), jnp.float32),
            pltpu.VMEM((slots, 8, rows), jnp.float32),
            pltpu.VMEM((2, slots, BLK, depth), jnp.float32),
            pltpu.VMEM((rows, depth), jnp.float32),
            pltpu.VMEM((depth, rows), jnp.bfloat16),
            pltpu.VMEM((depth, rows), jnp.bfloat16),
        ],
        compiler_params=pltpu.CompilerParams(vmem_limit_bytes=VMEM_BYTES),
        name="local_grads",
    )(block_pos, block_mask, query_rows, grad_rows,
      keys.reshape(slots, BLK, depth), values.reshape(slots, BLK, depth))


def reduce_kernel(members, planes, part_ref, out_ref, side, sums, landed, piece, swap,
                  side_send, side_recv, ring_send, ring_recv, pair_sem, own_sem,
                  z_send, z_recv, x_send, x_recv, twin_send, twin_recv):
    place = Place(members, planes)
    rows = part_ref.shape[2]
    half = rows // 2
    core = place.core
    pair_x = place.x + 1 - 2 * (place.x % 2)
    partner = place.head_id(place.z, pair_x, core)
    z_ids = [(place.z + step) % planes for step in range(1, planes)]
    x_ids = [(place.x + step) % X for step in range(1, X)]
    meet(
        [place.sibling()]
        + [place.along_y(steps) for steps in (1, -1, 2, -2)]
        + [place.head_id(place.z, x, core) for x in x_ids]
        + [place.head_id(z, place.x, core) for z in z_ids]
    )
    started = []

    def start(copy):
        copy.start()
        started.append(copy)

    offsets = [4, 3, -3, 1, -1, 2, -2, 0]

    def side_copy(steps):
        at = place.member(steps)
        slot = offsets.index(steps)
        return remote(part_ref.at[1 - core, at], side.at[slot], side_send.at[slot], side_recv.at[slot], place.sibling())

    for steps in offsets:
        start(side_copy(steps))

    def base(steps, which):
        slot = offsets.index(steps)
        at = place.member(steps)
        rows_at = pl.ds(which * half, half)
        return (part_ref[core, at, rows_at, :].astype(jnp.float32)
                + side[slot, rows_at, :].astype(jnp.float32))

    def ring_copy(way, reach, which, steps):
        return remote(
            sums.at[way, reach - 1, which],
            landed.at[way, reach - 1, which],
            ring_send.at[way, reach - 1, which],
            ring_recv.at[way, reach - 1, which],
            place.along_y((1 - 2 * way) * steps),
        )

    def arrived(way, reach, which):
        ring_copy(way, reach, which, 1).wait_recv()
        return landed[way, reach - 1, which].astype(jnp.float32)

    def send(way, reach, which, steps, value):
        sums[way, reach - 1, which] = value.astype(sums.dtype)
        start(ring_copy(way, reach, which, steps))

    def owner(way, reach):
        return 4 if reach == 4 else (1 - 2 * way) * reach

    side_copy(4).wait_recv()
    for way in range(2):
        send(way, 4, way, 2, base(4, way))
    for reach in (3, 1):
        for way in range(2):
            side_copy(owner(way, reach)).wait_recv()
            for which in range(2):
                send(way, reach, which, 1, base(owner(way, reach), which))
    for way in range(2):
        side_copy(owner(way, 2)).wait_recv()
        send(way, 2, 1 - way, 2, base(owner(way, 2), 1 - way) + arrived(way, 3, 1 - way))
    for way in range(2):
        send(way, 2, way, 2, base(owner(way, 2), way) + arrived(way, 3, way) + arrived(way, 4, way))
    side_copy(0).wait_recv()
    keep = place.x % 2

    for way in range(2):
        for reach in (1, 2):
            for which in range(2):
                ring_copy(way, reach, which, 1).wait_recv()

    def total(which):
        value = base(0, which)
        for way in range(2):
            for reach in (1, 2):
                value = value + landed[way, reach - 1, which].astype(jnp.float32)
        return value

    swap[0] = total(1 - keep).astype(swap.dtype)
    swap_copy = remote(swap.at[0], swap.at[1], pair_sem.at[0], pair_sem.at[1], partner)
    start(swap_copy)
    kept = total(keep)
    swap_copy.wait_recv()
    piece[...] = (kept + swap[1].astype(jnp.float32)).astype(piece.dtype)

    def spot(tensor, z, x):
        return out_ref.at[tensor, z * (X // 2) + x // 2, pl.ds(x % 2 * half, half)]

    here = spot(core, place.z, place.x)
    for number, z in enumerate(z_ids):
        start(remote(piece, here, z_send.at[number], z_recv.at[number], place.head_id(z, place.x, core)))
    for number, x in enumerate(x_ids):
        start(remote(piece, here, x_send.at[0, number], x_recv.at[0, number], place.head_id(place.z, x, core)))
    start(remote(piece, here, twin_send.at[0, 0], twin_recv.at[0, 0], place.sibling()))
    own = pltpu.make_async_copy(piece, here, own_sem)
    own.start()

    def landing(sem_send, sem_recv, spot_at):
        remote(spot_at, spot_at, sem_send, sem_recv, place.sibling()).wait_recv()

    def pass_on(number, index, x):
        spot_at = spot(core, (place.z - number + planes) % planes, x)
        landing(x_send.at[number, index], x_recv.at[number, index], spot_at)
        start(remote(spot_at, spot_at, twin_send.at[number, index + 1], twin_recv.at[number, index + 1],
                     place.sibling()))

    for number in range(planes - 1):
        z = (place.z - number - 1 + planes) % planes
        spot_at = spot(core, z, place.x)
        landing(z_send.at[number], z_recv.at[number], spot_at)
        for index, x in enumerate(x_ids):
            start(remote(spot_at, spot_at, x_send.at[number + 1, index], x_recv.at[number + 1, index],
                         place.head_id(place.z, x, core)))
        start(remote(spot_at, spot_at, twin_send.at[number + 1, 0], twin_recv.at[number + 1, 0], place.sibling()))
    for number in range(planes):
        for index in range(X - 1):
            pass_on(number, index, (place.x - index - 1 + X) % X)
    for number in range(planes):
        z = (place.z - number + planes) % planes
        for index in range(X):
            x = (place.x - index + X) % X
            landing(twin_send.at[number, index], twin_recv.at[number, index], spot(1 - core, z, x))
    own.wait()
    for copy in started:
        copy.wait_send()


def reduce_sums(members, planes, kv_count, partial_sums):
    _, slots, _, depth = partial_sums.shape
    rows = slots // members * BLK
    half = rows // 2
    dma = pltpu.SemaphoreType.DMA
    low = jnp.bfloat16
    return pl.pallas_call(
        functools.partial(reduce_kernel, members, planes),
        out_shape=pltpu.VMEM((2, kv_count, rows, depth), low),
        in_specs=[pl.BlockSpec(memory_space=pltpu.VMEM)],
        out_specs=pl.BlockSpec(memory_space=pltpu.VMEM),
        scratch_shapes=[
            pltpu.VMEM((members, rows, depth), low),
            pltpu.VMEM((2, 4, 2, half, depth), low),
            pltpu.VMEM((2, 4, 2, half, depth), low),
            pltpu.VMEM((half, depth), low),
            pltpu.VMEM((2, half, depth), low),
            dma((members,)),
            dma((members,)),
            dma((2, 4, 2)),
            dma((2, 4, 2)),
            dma((2,)),
            dma,
            dma((max(planes - 1, 1),)),
            dma((max(planes - 1, 1),)),
            dma((planes, X - 1)),
            dma((planes, X - 1)),
            dma((planes, X)),
            dma((planes, X)),
        ],
        compiler_params=pltpu.CompilerParams(
            collective_id=1, has_side_effects=True, vmem_limit_bytes=SMALL_VMEM_BYTES
        ),
        name="reduce_sums",
    )(partial_sums.reshape(2, members, rows, depth))


def per_device(queries, keys, values, d_out, block_pos, block_mask):
    members = lax.axis_size("ctx") // SEQS
    planes = lax.axis_size("head") // (CORES * X)
    tokens, heads, depth = queries.shape
    kv_count = keys.shape[1]
    key_all, value_all = gather(
        members, planes, jnp.transpose(keys, (1, 0, 2)), jnp.transpose(values, (1, 0, 2))
    )
    d_queries, partial_sums = local_grads(
        members,
        block_pos,
        block_mask,
        queries.reshape(tokens * heads, depth),
        d_out.reshape(tokens * heads, depth),
        key_all,
        value_all,
    )
    summed = reduce_sums(members, planes, kv_count, partial_sums)
    return (
        d_queries.reshape(tokens, heads, depth),
        jnp.transpose(summed[0], (1, 0, 2)),
        jnp.transpose(summed[1], (1, 0, 2)),
    )


def solution(mesh):
    placed = (
        P("ctx", "head", None),
        P("ctx", None, None),
        P("ctx", None, None),
        P("ctx", "head", None),
        P(),
        P(),
    )
    return jax.shard_map(
        per_device,
        mesh=mesh,
        in_specs=placed,
        out_specs=(P("ctx", "head", None), P("ctx", None, None), P("ctx", None, None)),
        check_vma=False,
    )
```

time: 105 us -> 96.9 us (0.923); the launches traced: 105 us -> 95.3 us
  Pallas kernels: 101 us -> 91 us
    pallas_call x1, Pallas kernels: 57.1 us -> 50.3 us  [reduce_sums(): pl.pallas_call(functools.partial(reduce_kernel, members, planes), out_sha...]
    pallas_call x1, Pallas kernels: 30.6 us -> 25.5 us  [gather(): pl.pallas_call(functools.partial(gather_kernel, members, planes, kv_count...]
    unnamed x0 -> x12, local copies, waits for them, and re-layouts: none -> 2.28 us
    pallas_call x1, Pallas kernels: 13.7 us -> 15.2 us  [local_grads(): pl.pallas_call(functools.partial(grad_kernel, members), out_shape=(jax.Sh...]
    transpose x1, local copies, waits for them, and re-layouts: 2.61 us -> 1.24 us  [per_device(): jnp.transpose(summed[1], (1, 0, 2))]
where the time goes in v2:
time: 96.9 us; the launch traced here: 95.3 us
  Pallas kernels  91 us (94%)
  local copies, waits for them, and re-layouts  3.52 us (4%)
    pallas_call x1, Pallas kernels, reduce_sums(): pl.pallas_call(functools.partial(reduce_kernel, members, planes), out_sha...  50.3 us
    pallas_call x1, Pallas kernels, gather(): pl.pallas_call(functools.partial(gather_kernel, members, planes, kv_count...  25.5 us
    pallas_call x1, Pallas kernels, local_grads(): pl.pallas_call(functools.partial(grad_kernel, members), out_shape=(jax.Sh...  15.2 us
    unnamed x12, local copies, waits for them, and re-layouts  2.28 us

profile of v2, /device:TPU:1, one launch (start us, length us, event | category | flops | bytes accessed | tf_op | source)
XLA Modules:
  0.0 95.3 jit_solution(12170518487922169091)
XLA Ops:
  0.6 0.0 copy-start.5
  0.6 0.0 copy-start
  0.7 1.1 %copy-done = bf16[512,6,128]{2,0,1:T(8,128)(2,1)S(1)} copy-done((bf16[512,6,128]{2,0,1:T(8,128)(2,1)S(1)}, bf16[512,6,128]{2,0,1:T(8,128)(2,1)}, u32[]{:S(2)}) %copy-start) | copy-done | bytes 786456
  1.8 0.0 copy-start.1
  1.8 1.1 %copy-done.1 = bf16[512,6,128]{2,0,1:T(8,128)(2,1)S(1)} copy-done((bf16[512,6,128]{2,0,1:T(8,128)(2,1)S(1)}, bf16[512,6,128]{2,0,1:T(8,128)(2,1)}, u32[]{:S(2)}) %copy-start.1) | copy-done | bytes 786456
  2.9 0.0 copy-start.2
  2.9 0.0 copy-start.3
  2.9 0.0 copy-start.4
  2.9 25.5 %gather_keys.1 = (bf16[8,512,128]{2,1,0:T(8,128)(2,1)S(1)}, bf16[8,512,128]{2,1,0:T(8,128)(2,1)S(1)}) custom-call(bf16[6,512,128]{2,1,0:T(8,128)(2,1)S(1)} %bitcast.19, bf16[6,512,128]{2,1,0:T(8,128)(2,1)S(1)} %bitcast.20), custom_call_target="tpu_custom_call" | custom-call | tf_op jit(solution)/shard_map/gather_keys/pallas_call | solution.py:137
  28.5 0.0 copy-done.5
  28.5 0.0 copy-done.2
  28.5 0.0 copy-done.3
  28.5 0.0 copy-done.4
  28.5 15.2 %local_grads.1 = (bf16[2048,128]{1,0:T(8,128)(2,1)}, bf16[2,32,128,128]{3,2,1,0:T(8,128)(2,1)S(1)}) custom-call(s32[4,32]{1,0:T(4,128)S(1)} %copy-done.5, s32[4,32,32]{2,1,0:T(8,128)S(1)} %copy-done.4, bf16[2048,128]{1,0:T(8,128)(2,1)S(1)} %bitcast.21, bf16[2048,128]{1,0:T(8,128)(2,1)S(1)} %bitcast.22, bf16[32,128,128]{2,1,0:T(8,128)(2,1)S(1)} %bitcast.17, ...), custom_call_target="tpu_custom_call" | custom-call | tf_op jit(solution)/shard_map/local_grads/pallas_call | solution.py:283
  43.7 50.3 %reduce_sums.1 = bf16[2,6,512,128]{3,2,1,0:T(8,128)(2,1)S(1)} custom-call(bf16[2,8,512,128]{3,2,1,0:T(8,128)(2,1)S(1)} %bitcast.16), custom_call_target="tpu_custom_call" | custom-call | tf_op jit(solution)/shard_map/reduce_sums/pallas_call | solution.py:450
  94.0 1.2 %slice_bitcast_fusion = (bf16[512,6,128]{2,0,1:T(8,128)(2,1)}, bf16[512,6,128]{2,0,1:T(8,128)(2,1)}) fusion(bf16[2,6,512,128]{3,2,1,0:T(8,128)(2,1)S(1)} %reduce_sums.1), kind=kLoop, calls=%fused_computation | loop fusion | bytes 3145728 | tf_op jit(solution)/shard_map/transpose | solution.py:502
Async XLA Ops:
  0.6 27.8 %copy-start.5 = (s32[4,32]{1,0:T(4,128)S(1)}, s32[4,32]{1,0:T(4,128)}, u32[]{:S(2)}) copy-start(s32[4,32]{1,0:T(4,128)} %order_ref.1) | copy-start | bytes 1540
  0.6 1.1 %copy-start = (bf16[512,6,128]{2,0,1:T(8,128)(2,1)S(1)}, bf16[512,6,128]{2,0,1:T(8,128)(2,1)}, u32[]{:S(2)}) copy-start(bf16[512,6,128]{2,0,1:T(8,128)(2,1)} %param.7) | copy-start | bytes 2359300
  1.8 1.1 %copy-start.1 = (bf16[512,6,128]{2,0,1:T(8,128)(2,1)S(1)}, bf16[512,6,128]{2,0,1:T(8,128)(2,1)}, u32[]{:S(2)}) copy-start(bf16[512,6,128]{2,0,1:T(8,128)(2,1)} %param.8) | copy-start | bytes 2359300
  2.9 25.6 %copy-start.2 = (bf16[512,4,128]{2,1,0:T(4,128)(2,1)S(1)}, bf16[512,4,128]{2,1,0:T(4,128)(2,1)}, u32[]{:S(2)}) copy-start(bf16[512,4,128]{2,1,0:T(4,128)(2,1)} %param.6) | copy-start | bytes 1572868
  2.9 25.6 %copy-start.3 = (bf16[512,4,128]{2,1,0:T(4,128)(2,1)S(1)}, bf16[512,4,128]{2,1,0:T(4,128)(2,1)}, u32[]{:S(2)}) copy-start(bf16[512,4,128]{2,1,0:T(4,128)(2,1)} %param.9) | copy-start | bytes 1572868
  2.9 25.6 %copy-start.4 = (s32[4,32,32]{2,1,0:T(8,128)S(1)}, s32[4,32,32]{2,1,0:T(8,128)}, u32[]{:S(2)}) copy-start(s32[4,32,32]{2,1,0:T(8,128)} %mask_ref.1) | copy-start | bytes 49156

commit v3 on v2

--- a/solution.py
+++ b/solution.py
@@ -137,7 +137,7 @@
     return pl.pallas_call(
         functools.partial(gather_kernel, members, planes, kv_count // planes),
         out_shape=(out, out),
-        in_specs=[pl.BlockSpec(memory_space=pl.ANY)] * 2,
+        in_specs=[pl.BlockSpec(memory_space=pltpu.HBM)] * 2,
         out_specs=[pl.BlockSpec(memory_space=pltpu.VMEM)] * 2,
         scratch_shapes=[pltpu.SemaphoreType.DMA((2,))]
         + [pltpu.SemaphoreType.DMA((2, 2, members // 2))] * 4,
@@ -145,7 +145,7 @@
             collective_id=0, has_side_effects=True, vmem_limit_bytes=SMALL_VMEM_BYTES
         ),
         name="gather_keys",
-    )(keys, values)
+    )(pltpu.with_memory_space_constraint(keys, pltpu.HBM), pltpu.with_memory_space_constraint(values, pltpu.HBM))
 
 
 def dot(left, right):
@@ -304,15 +304,15 @@
       keys.reshape(slots, BLK, depth), values.reshape(slots, BLK, depth))
 
 
-def reduce_kernel(members, planes, part_ref, out_ref, side, sums, landed, piece, swap,
-                  side_send, side_recv, ring_send, ring_recv, pair_sem, own_sem,
+def reduce_kernel(members, planes, part_ref, out_ref, side, give, given, sums, landed, piece,
+                  side_send, side_recv, pair_send, pair_recv, ring_send, ring_recv, own_sem,
                   z_send, z_recv, x_send, x_recv, twin_send, twin_recv):
     place = Place(members, planes)
-    rows = part_ref.shape[2]
-    half = rows // 2
+    half = part_ref.shape[2] // 2
+    quarter = half // 2
     core = place.core
-    pair_x = place.x + 1 - 2 * (place.x % 2)
-    partner = place.head_id(place.z, pair_x, core)
+    keep = place.x % 2
+    partner = place.head_id(place.z, place.x + 1 - 2 * keep, core)
     z_ids = [(place.z + step) % planes for step in range(1, planes)]
     x_ids = [(place.x + step) % X for step in range(1, X)]
     meet(
@@ -334,79 +334,73 @@
         slot = offsets.index(steps)
         return remote(part_ref.at[1 - core, at], side.at[slot], side_send.at[slot], side_recv.at[slot], place.sibling())
 
+    def pair_copy(steps):
+        slot = offsets.index(steps)
+        return remote(give.at[slot], given.at[slot], pair_send.at[slot], pair_recv.at[slot], partner)
+
+    def chip_sum(steps, which):
+        rows_at = pl.ds(pl.multiple_of(which * half, half), half)
+        return (part_ref[core, place.member(steps), rows_at, :].astype(jnp.float32)
+                + side[offsets.index(steps), rows_at, :].astype(jnp.float32))
+
+    def pair_sum(steps):
+        pair_copy(steps).wait_recv()
+        return chip_sum(steps, keep) + given[offsets.index(steps)].astype(jnp.float32)
+
+    def ring_copy(way, reach, steps):
+        rows_at = pl.ds(way * quarter, quarter) if reach == 4 else pl.ds(0, half)
+        return remote(
+            sums.at[way, reach - 1, rows_at],
+            landed.at[way, reach - 1, rows_at],
+            ring_send.at[way, reach - 1],
+            ring_recv.at[way, reach - 1],
+            place.along_y((1 - 2 * way) * steps),
+        )
+
+    def send(way, reach, steps, value):
+        sums[way, reach - 1] = value.astype(sums.dtype)
+        start(ring_copy(way, reach, steps))
+
     for steps in offsets:
         start(side_copy(steps))
-
-    def base(steps, which):
-        slot = offsets.index(steps)
-        at = place.member(steps)
-        rows_at = pl.ds(which * half, half)
-        return (part_ref[core, at, rows_at, :].astype(jnp.float32)
-                + side[slot, rows_at, :].astype(jnp.float32))
-
-    def ring_copy(way, reach, which, steps):
-        return remote(
-            sums.at[way, reach - 1, which],
-            landed.at[way, reach - 1, which],
-            ring_send.at[way, reach - 1, which],
-            ring_recv.at[way, reach - 1, which],
-            place.along_y((1 - 2 * way) * steps),
-        )
-
-    def arrived(way, reach, which):
-        ring_copy(way, reach, which, 1).wait_recv()
-        return landed[way, reach - 1, which].astype(jnp.float32)
-
-    def send(way, reach, which, steps, value):
-        sums[way, reach - 1, which] = value.astype(sums.dtype)
-        start(ring_copy(way, reach, which, steps))
-
-    def owner(way, reach):
-        return 4 if reach == 4 else (1 - 2 * way) * reach
-
-    side_copy(4).wait_recv()
+    for steps in offsets:
+        side_copy(steps).wait_recv()
+        give[offsets.index(steps)] = chip_sum(steps, 1 - keep).astype(give.dtype)
+        start(pair_copy(steps))
+    far = pair_sum(4)
     for way in range(2):
-        send(way, 4, way, 2, base(4, way))
+        send(way, 4, 2, far)
     for reach in (3, 1):
         for way in range(2):
-            side_copy(owner(way, reach)).wait_recv()
-            for which in range(2):
-                send(way, reach, which, 1, base(owner(way, reach), which))
+            send(way, reach, 1, pair_sum((1 - 2 * way) * reach))
     for way in range(2):
-        side_copy(owner(way, 2)).wait_recv()
-        send(way, 2, 1 - way, 2, base(owner(way, 2), 1 - way) + arrived(way, 3, 1 - way))
-    for way in range(2):
-        send(way, 2, way, 2, base(owner(way, 2), way) + arrived(way, 3, way) + arrived(way, 4, way))
-    side_copy(0).wait_recv()
-    keep = place.x % 2
-
-    for way in range(2):
-        for reach in (1, 2):
-            for which in range(2):
-                ring_copy(way, reach, which, 1).wait_recv()
-
-    def total(which):
-        value = base(0, which)
+        value = pair_sum((1 - 2 * way) * 2)
+        ring_copy(way, 3, 1).wait_recv()
+        value = value + landed[way, 2].astype(jnp.float32)
+        ring_copy(way, 4, 2).wait_recv()
+        late = value[way * quarter:(way + 1) * quarter] + landed[
+            way, 3, way * quarter:(way + 1) * quarter].astype(jnp.float32)
+        early = value[(1 - way) * quarter:(2 - way) * quarter]
+        send(way, 2, 2, jnp.concatenate([early, late] if way else [late, early], axis=0))
+    value = pair_sum(0)
+    for reach in (1, 2):
         for way in range(2):
-            for reach in (1, 2):
-                value = value + landed[way, reach - 1, which].astype(jnp.float32)
-        return value
-
-    swap[0] = total(1 - keep).astype(swap.dtype)
-    swap_copy = remote(swap.at[0], swap.at[1], pair_sem.at[0], pair_sem.at[1], partner)
-    start(swap_copy)
-    kept = total(keep)
-    swap_copy.wait_recv()
-    piece[...] = (kept + swap[1].astype(jnp.float32)).astype(piece.dtype)
-
-    def spot(tensor, z, x):
-        return out_ref.at[tensor, z * (X // 2) + x // 2, pl.ds(x % 2 * half, half)]
+            ring_copy(way, reach, 1).wait_recv()
+            value = value + landed[way, reach - 1].astype(jnp.float32)
+    piece[...] = value.astype(piece.dtype)
+
+    def spot(tensor, z, x, sub=None):
+        start_at, size = (0, half) if sub is None else (sub * quarter, quarter)
+        rows_at = pl.ds(pl.multiple_of(x % 2 * half + start_at, size), size)
+        return out_ref.at[tensor, z * (X // 2) + x // 2, rows_at]
 
     here = spot(core, place.z, place.x)
-    for number, z in enumerate(z_ids):
-        start(remote(piece, here, z_send.at[number], z_recv.at[number], place.head_id(z, place.x, core)))
+    for sub in range(2):
+        for number, z in enumerate(z_ids):
+            start(remote(piece.at[pl.ds(sub * quarter, quarter)], spot(core, place.z, place.x, sub),
+                         z_send.at[number, sub], z_recv.at[number, sub], place.head_id(z, place.x, core)))
     for number, x in enumerate(x_ids):
-        start(remote(piece, here, x_send.at[0, number], x_recv.at[0, number], place.head_id(place.z, x, core)))
+        start(remote(piece, here, x_send.at[0, number, 0], x_recv.at[0, number, 0], place.head_id(place.z, x, core)))
     start(remote(piece, here, twin_send.at[0, 0], twin_recv.at[0, 0], place.sibling()))
     own = pltpu.make_async_copy(piece, here, own_sem)
     own.start()
@@ -414,28 +408,33 @@
     def landing(sem_send, sem_recv, spot_at):
         remote(spot_at, spot_at, sem_send, sem_recv, place.sibling()).wait_recv()
 
-    def pass_on(number, index, x):
-        spot_at = spot(core, (place.z - number + planes) % planes, x)
-        landing(x_send.at[number, index], x_recv.at[number, index], spot_at)
-        start(remote(spot_at, spot_at, twin_send.at[number, index + 1], twin_recv.at[number, index + 1],
-                     place.sibling()))
-
-    for number in range(planes - 1):
-        z = (place.z - number - 1 + planes) % planes
-        spot_at = spot(core, z, place.x)
-        landing(z_send.at[number], z_recv.at[number], spot_at)
-        for index, x in enumerate(x_ids):
-            start(remote(spot_at, spot_at, x_send.at[number + 1, index], x_recv.at[number + 1, index],
-                         place.head_id(place.z, x, core)))
-        start(remote(spot_at, spot_at, twin_send.at[number + 1, 0], twin_recv.at[number + 1, 0], place.sibling()))
+    def from_plane(number):
+        return (place.z - number + planes) % planes
+
+    def to_twin(number, index, x):
+        spot_at = spot(core, from_plane(number), x)
+        start(remote(spot_at, spot_at, twin_send.at[number, index], twin_recv.at[number, index], place.sibling()))
+
+    for sub in range(2):
+        for number in range(1, planes):
+            spot_at = spot(core, from_plane(number), place.x, sub)
+            landing(z_send.at[number - 1, sub], z_recv.at[number - 1, sub], spot_at)
+            for index, x in enumerate(x_ids):
+                start(remote(spot_at, spot_at, x_send.at[number, index, sub], x_recv.at[number, index, sub],
+                             place.head_id(place.z, x, core)))
+    for number in range(1, planes):
+        to_twin(number, 0, place.x)
     for number in range(planes):
         for index in range(X - 1):
-            pass_on(number, index, (place.x - index - 1 + X) % X)
+            x = (place.x - index - 1 + X) % X
+            for sub in range(2) if number else (None,):
+                landing(x_send.at[number, index, sub or 0], x_recv.at[number, index, sub or 0],
+                        spot(core, from_plane(number), x, sub))
+            to_twin(number, index + 1, x)
     for number in range(planes):
-        z = (place.z - number + planes) % planes
         for index in range(X):
             x = (place.x - index + X) % X
-            landing(twin_send.at[number, index], twin_recv.at[number, index], spot(1 - core, z, x))
+            landing(twin_send.at[number, index], twin_recv.at[number, index], spot(1 - core, from_plane(number), x))
     own.wait()
     for copy in started:
         copy.wait_send()
@@ -447,6 +446,7 @@
     half = rows // 2
     dma = pltpu.SemaphoreType.DMA
     low = jnp.bfloat16
+    z_count = max(planes - 1, 1)
     return pl.pallas_call(
         functools.partial(reduce_kernel, members, planes),
         out_shape=pltpu.VMEM((2, kv_count, rows, depth), low),
@@ -454,20 +454,22 @@
         out_specs=pl.BlockSpec(memory_space=pltpu.VMEM),
         scratch_shapes=[
             pltpu.VMEM((members, rows, depth), low),
-            pltpu.VMEM((2, 4, 2, half, depth), low),
-            pltpu.VMEM((2, 4, 2, half, depth), low),
+            pltpu.VMEM((members, half, depth), low),
+            pltpu.VMEM((members, half, depth), low),
+            pltpu.VMEM((2, 4, half, depth), low),
+            pltpu.VMEM((2, 4, half, depth), low),
             pltpu.VMEM((half, depth), low),
-            pltpu.VMEM((2, half, depth), low),
             dma((members,)),
             dma((members,)),
-            dma((2, 4, 2)),
-            dma((2, 4, 2)),
-            dma((2,)),
+            dma((members,)),
+            dma((members,)),
+            dma((2, 4)),
+            dma((2, 4)),
             dma,
-            dma((max(planes - 1, 1),)),
-            dma((max(planes - 1, 1),)),
-            dma((planes, X - 1)),
-            dma((planes, X - 1)),
+            dma((z_count, 2)),
+            dma((z_count, 2)),
+            dma((planes, X - 1, 2)),
+            dma((planes, X - 1, 2)),
             dma((planes, X)),
             dma((planes, X)),
         ],

time: 96.9 us -> 92.7 us (0.957); the launches traced: 95.3 us -> 92.5 us
  local copies, waits for them, and re-layouts: 3.52 us -> 1.26 us
    pallas_call x1, Pallas kernels: 15.2 us -> 12.5 us  [local_grads(): pl.pallas_call(functools.partial(grad_kernel, members), out_shape=(jax.Sh...]
    unnamed x12 -> x8, local copies, waits for them, and re-layouts: 2.28 us -> 0.02 us
    pallas_call x1, Pallas kernels: 50.3 us -> 52.2 us  [reduce_sums(): pl.pallas_call(functools.partial(reduce_kernel, members, planes), out_sha...]
where the time goes in v3:
time: 92.7 us; the launch traced here: 92.5 us
  Pallas kernels  90.5 us (98%)
  local copies, waits for them, and re-layouts  1.26 us (1%)
    pallas_call x1, Pallas kernels, reduce_sums(): pl.pallas_call(functools.partial(reduce_kernel, members, planes), out_sha...  52.2 us
    pallas_call x1, Pallas kernels, gather(): pl.pallas_call(functools.partial(gather_kernel, members, planes, kv_count...  25.8 us
    pallas_call x1, Pallas kernels, local_grads(): pl.pallas_call(functools.partial(grad_kernel, members), out_shape=(jax.Sh...  12.5 us

profile of v3, /device:TPU:1, one launch (start us, length us, event | category | flops | bytes accessed | tf_op | source)
XLA Modules:
  0.0 92.5 jit_solution(1237579453094423212)
XLA Ops:
  0.6 0.0 copy-start.2
  0.6 0.0 copy-start.3
  0.7 0.0 copy-start.1
  0.7 0.0 copy-start
  0.7 25.8 %gather_keys.1 = (bf16[8,512,128]{2,1,0:T(8,128)(2,1)S(1)}, bf16[8,512,128]{2,1,0:T(8,128)(2,1)S(1)}) custom-call(bf16[6,512,128]{2,1,0:T(8,128)(2,1)} %bitcast.21, bf16[6,512,128]{2,1,0:T(8,128)(2,1)} %bitcast.22), custom_call_target="tpu_custom_call" | custom-call | tf_op jit(solution)/shard_map/gather_keys/pallas_call | solution.py:137
  26.4 0.0 copy-done.2
  26.4 0.0 copy-done.3
  26.5 0.0 copy-done.1
  26.5 0.0 copy-done
  26.5 12.5 %local_grads.1 = (bf16[2048,128]{1,0:T(8,128)(2,1)}, bf16[2,32,128,128]{3,2,1,0:T(8,128)(2,1)S(1)}) custom-call(s32[4,32]{1,0:T(4,128)S(1)} %copy-done.3, s32[4,32,32]{2,1,0:T(8,128)S(1)} %copy-done.2, bf16[2048,128]{1,0:T(8,128)(2,1)S(1)} %bitcast.19, bf16[2048,128]{1,0:T(8,128)(2,1)S(1)} %bitcast.20, bf16[32,128,128]{2,1,0:T(8,128)(2,1)S(1)} %bitcast.17, ...), custom_call_target="tpu_custom_call" | custom-call | tf_op jit(solution)/shard_map/local_grads/pallas_call | solution.py:283
  39.0 52.2 %reduce_sums.1 = bf16[2,6,512,128]{3,2,1,0:T(8,128)(2,1)S(1)} custom-call(bf16[2,8,512,128]{3,2,1,0:T(8,128)(2,1)S(1)} %bitcast.16), custom_call_target="tpu_custom_call" | custom-call | tf_op jit(solution)/shard_map/reduce_sums/pallas_call | solution.py:450
  91.3 1.2 %slice_bitcast_fusion = (bf16[512,6,128]{2,0,1:T(8,128)(2,1)}, bf16[512,6,128]{2,0,1:T(8,128)(2,1)}) fusion(bf16[2,6,512,128]{3,2,1,0:T(8,128)(2,1)S(1)} %reduce_sums.1), kind=kLoop, calls=%fused_computation | loop fusion | bytes 3145728 | tf_op jit(solution)/shard_map/transpose | solution.py:504
Async XLA Ops:
  0.6 25.8 %copy-start.2 = (s32[4,32,32]{2,1,0:T(8,128)S(1)}, s32[4,32,32]{2,1,0:T(8,128)}, u32[]{:S(2)}) copy-start(s32[4,32,32]{2,1,0:T(8,128)} %mask_ref.1) | copy-start | bytes 49156
  0.6 25.8 %copy-start.3 = (s32[4,32]{1,0:T(4,128)S(1)}, s32[4,32]{1,0:T(4,128)}, u32[]{:S(2)}) copy-start(s32[4,32]{1,0:T(4,128)} %order_ref.1) | copy-start | bytes 1540
  0.7 25.8 %copy-start.1 = (bf16[512,4,128]{2,1,0:T(4,128)(2,1)S(1)}, bf16[512,4,128]{2,1,0:T(4,128)(2,1)}, u32[]{:S(2)}) copy-start(bf16[512,4,128]{2,1,0:T(4,128)(2,1)} %param.9) | copy-start | bytes 1572868
  0.7 25.8 %copy-start = (bf16[512,4,128]{2,1,0:T(4,128)(2,1)S(1)}, bf16[512,4,128]{2,1,0:T(4,128)(2,1)}, u32[]{:S(2)}) copy-start(bf16[512,4,128]{2,1,0:T(4,128)(2,1)} %param.6) | copy-start | bytes 1572868
